TPU v7x, 768 devices: a whole 4x8x12 slice. The times are simulated.
768 devices in a mesh: comp: 2 (over core), blk: 48 (over z, x), sub: 8 (over y).
Axes of the slice: x: 4, y: 8, z: 12, core: 2. Of those that a mesh axis runs over, the one named last changes fastest.
Arguments:
- ocean_state: float32 [3, 256, 12288], P(None, ('comp', 'sub'), 'blk'), may hold values from -4 to 4
- sea_temp: float32 [256, 12288], P(('comp', 'sub'), 'blk'), may hold values from -6 to 6
- land_mask: int32 [256, 12288], P(('comp', 'sub'), 'blk'), may hold values from 0 to 1, as said below
- atm_flux: bfloat16 [16, 3072, 12, 128], P(('comp', 'sub'), 'blk'), may hold values from -6 to 6
- remap_w: bfloat16 [256, 96, 3, 128, 128], P(('comp', 'sub'), 'blk'), may hold values from -0.3125 to 0.3125
- source_tile: int32 [256, 96, 3], P(('comp', 'sub'), 'blk'), may hold values from 0 to 3071, as said below
- send_tiles: int32 [16, 48, 48, 3], P(('comp', 'sub'), 'blk'), may hold values from -1 to 63, as said below
- flux_mix: float32 [3, 12], replicated, may hold values from -1.75 to 1.75
Outputs:
- ocean_out: float32 [3, 256, 12288], P(None, ('comp', 'sub'), 'blk')
- atm_surface: float32 [16, 3072, 2, 128], P(('comp', 'sub'), 'blk')
Inputs may be any that keep to these rules, and one draw needn't show every extreme that they name: `source_tile`: each entry names a tile of the ocean tile's own band; value // 64 is the index along blk of the device that holds it. send_tiles[b, j, k] lists, in ascending order, the distinct tiles value % 64 of the source_tile entries of ocean block k of band b with value // 64 = j, followed by -1; every band has, for each j, some k, and for each k, some j, with all 3 filled. `land_mask`: the first and last rows of the grid are land.
All inputs are finite; a program needn't handle non-finite values.
Results may differ from a plain program's by a relative error of at most 0.0025.
Values may be sent and summed in bfloat16 or wider, within the bound.
A program may use at most 64 MiB of HBM per device.

v0:
```python
import jax
import jax.numpy as jnp
from jax import lax
from jax.sharding import PartitionSpec as P

SUBCYCLES = 10


drag_rate = 0.02
gravity_step = 0.6
depth_step = 0.6
force_step = 0.1
spread_rate = 0.1
filter_rate = 0.1


def padded(shard, sides, width):
    for axis, dim in sides:
        size, length = (lax.axis_size(axis), shard.shape[dim])
        up = [(i, (i + 1) % size) for i in range(size)]
        down = [(j, i) for i, j in up]
        last = lax.slice_in_dim(shard, length - width, length, axis=dim)
        first = lax.slice_in_dim(shard, 0, width, axis=dim)
        before = lax.ppermute(last, axis, up)
        after = lax.ppermute(first, axis, down)
        shard = jnp.concatenate([before, shard, after], axis=dim)
    return shard


def shards(ocean_state, sea_temp, land_mask, atm_flux, remap_w, source_tile, send_tiles, flux_mix):
    blocks = lax.axis_size("blk")
    atm_tiles = atm_flux.shape[1]
    fields = atm_flux.shape[2]
    tile_cells = atm_flux.shape[3]
    capacity = send_tiles.shape[3]
    rows_dev, cols_dev = sea_temp.shape
    sources = remap_w.shape[2]
    ocean_tiles = rows_dev * cols_dev // tile_cells
    weights = remap_w.reshape(ocean_tiles, sources, tile_cells, tile_cells)
    ref_ids = source_tile.reshape(-1)
    ref_count = ref_ids.shape[0]
    owner_dev = ref_ids // atm_tiles
    positions = jnp.arange(ref_count)
    repeated = jnp.any(
        (ref_ids[:, None] == ref_ids[None, :]) & (positions[None, :] < positions[:, None]), axis=1
    )
    leading = jnp.logical_not(repeated)
    slot_pos = jnp.sum(
        leading[None, :]
        & (owner_dev[None, :] == owner_dev[:, None])
        & (ref_ids[None, :] < ref_ids[:, None]),
        axis=1,
    )
    arrival = owner_dev * capacity + slot_pos
    pick_table = arrival[:, None] == jnp.arange(blocks * capacity)[None, :]
    send_table = send_tiles.reshape(blocks * capacity)[:, None] == jnp.arange(atm_tiles)[None, :]
    row_width = fields * tile_cells
    shard_rows = lax.all_gather(atm_flux, "blk", axis=1, tiled=True)
    count_rows = shard_rows.shape[1]
    select = (ref_ids[:, None] == jnp.arange(count_rows)[None, :]).astype(jnp.bfloat16)
    picked = jnp.dot(
        select, shard_rows.reshape(count_rows, row_width), preferred_element_type=jnp.float32
    )
    picked = picked.astype(jnp.bfloat16)
    remapped = jnp.einsum(
        "tkao,tkfa->fto",
        weights,
        picked.reshape(ocean_tiles, sources, fields, tile_cells),
        preferred_element_type=jnp.float32,
    )
    remapped = remapped.reshape(fields, rows_dev, cols_dev)
    forcing = jnp.einsum("qf,fyx->qyx", flux_mix, remapped, precision=lax.Precision.HIGHEST)
    sea_cells = land_mask.astype(jnp.float32)
    sea_pad = padded(sea_cells, ((("comp", "sub"), 0), ("blk", 1)), 1)
    east_pad = sea_pad[:, :-1] * sea_pad[:, 1:]
    north_pad = sea_pad[:-1, :] * sea_pad[1:, :]
    east_open = east_pad[1:-1, 1:]
    west_open = east_pad[1:-1, :-1]
    north_open = north_pad[1:, 1:-1]
    south_open = north_pad[:-1, 1:-1]
    push_east = forcing[0]
    push_north = forcing[1]

    def advance(sub_step, carried):
        eta, east_vel, north_vel = carried
        heights = padded(eta, ((("comp", "sub"), 0), ("blk", 1)), 1)
        middle = heights[1:-1, 1:-1]
        east_vel = east_open * (
            (1.0 - drag_rate) * east_vel
            - gravity_step * (heights[1:-1, 2:] - middle)
            + force_step * push_east
        )
        north_vel = north_open * (
            (1.0 - drag_rate) * north_vel
            - gravity_step * (heights[2:, 1:-1] - middle)
            + force_step * push_north
        )
        moving = padded(jnp.stack([east_vel, north_vel]), ((("comp", "sub"), 1), ("blk", 2)), 1)
        spread = (
            east_open * (heights[1:-1, 2:] - middle)
            - west_open * (middle - heights[1:-1, :-2])
            + north_open * (heights[2:, 1:-1] - middle)
            - south_open * (middle - heights[:-2, 1:-1])
        )
        eta = sea_cells * (
            eta
            - depth_step
            * (
                moving[0, 1:-1, 1:-1]
                - moving[0, 1:-1, :-2]
                + moving[1, 1:-1, 1:-1]
                - moving[1, :-2, 1:-1]
            )
            + spread_rate * spread
        )
        beside_all = (
            moving[:, 1:-1, 2:]
            + moving[:, 1:-1, :-2]
            + moving[:, 2:, 1:-1]
            + moving[:, :-2, 1:-1]
            - 4.0 * moving[:, 1:-1, 1:-1]
        )
        east_vel = east_open * (east_vel + filter_rate * beside_all[0])
        north_vel = north_open * (north_vel + filter_rate * beside_all[1])
        return (eta, east_vel, north_vel)

    eta, east_vel, north_vel = lax.fori_loop(
        0, SUBCYCLES, advance, (ocean_state[0], ocean_state[1], ocean_state[2])
    )
    ocean_out = jnp.stack([eta, east_vel, north_vel])
    surface = sea_cells * (sea_temp + forcing[2])
    ice_cover = sea_cells * jax.nn.sigmoid(-2.0 * (surface + 1.0))
    returned = (
        jnp.stack([surface, ice_cover]).astype(jnp.bfloat16).reshape(2, ocean_tiles, tile_cells)
    )
    contrib = jnp.einsum(
        "tkao,fto->tkfa", weights, returned, preferred_element_type=jnp.float32
    ).reshape(ref_count, 2 * tile_cells)
    per_slot = jnp.dot(
        pick_table.astype(jnp.float32).T, contrib, precision=lax.Precision.HIGHEST
    ).reshape(blocks, capacity, 2 * tile_cells)
    came_back = lax.all_to_all(per_slot, "blk", split_axis=0, concat_axis=0, tiled=True)
    atm_surface = jnp.dot(
        send_table.astype(jnp.float32).T,
        came_back.reshape(blocks * capacity, 2 * tile_cells),
        precision=lax.Precision.HIGHEST,
    )
    return (ocean_out, atm_surface.reshape(1, atm_tiles, 2, tile_cells))


def solution(mesh):
    placed = (
        P(None, ("comp", "sub"), "blk"),
        P(("comp", "sub"), "blk"),
        P(("comp", "sub"), "blk"),
        P(("comp", "sub"), "blk", None, None),
        P(("comp", "sub"), "blk", None, None, None),
        P(("comp", "sub"), "blk", None),
        P(("comp", "sub"), "blk", None, None),
        P(),
    )
    return jax.shard_map(
        shards,
        mesh=mesh,
        in_specs=placed,
        out_specs=(P(None, ("comp", "sub"), "blk"), P(("comp", "sub"), "blk", None, None)),
        check_vma=False,
    )
```

profile of v0, /device:TPU:8, one launch (start us, length us, event | category | flops | bytes accessed | tf_op | source)
XLA Modules:
  0.0 651.7 jit_solution(1601160260209417460)
XLA Ops:
  8.8 3.5 collective-permute-start.8
  12.3 9.8 %collective-permute-start.9 = (f32[1,256]{1,0:T(1,128)S(1)}, f32[1,256]{1,0:T(1,128)S(1)}, u32[]{:S(2)}, u32[]{:S(2)}) collective-permute-start(f32[1,256]{1,0:T(1,128)S(1)} %get-tuple-element.121), channel_id=1, source_target_pairs={{1,0},{2,1},{3,2},{4,3},{5,4},{6,5},{7,6},{384,7},{385,384},{386,3... | collective-permute-start | bytes 3080 | tf_op jit(solution)/shard_map/ppermute | solution.py:25
  27.5 9.3 %collective-permute-start.11 = (f32[18,1]{1,0:T(8,128)S(1)}, f32[18,1]{1,0:T(8,128)S(1)}, u32[]{:S(2)}, u32[]{:S(2)}) collective-permute-start(f32[18,1]{1,0:T(8,128)S(1)} %get-tuple-element.118), channel_id=1, source_target_pairs={{8,0},{16,8},{24,16},{32,24},{40,32},{48,40},{56,48},{64,56},{72,6... | collective-permute-start | bytes 224 | tf_op jit(solution)/shard_map/ppermute | solution.py:25
  38.8 7.0 %collective-permute-done.10 = f32[18,1]{1,0:T(8,128)S(1)} collective-permute-done((f32[18,1]{1,0:T(8,128)S(1)}, f32[18,1]{1,0:T(8,128)S(1)}, u32[]{:S(2)}, u32[]{:S(2)}) %collective-permute-start.10) | collective-permute-done | bytes 104 | tf_op jit(solution)/shard_map/ppermute | solution.py:24
  46.0 109.7 %all-gather.2.cloned.1.call-done = bf16[1,3072,12,128]{3,1,2,0:T(8,128)(2,1)} async-done(((bf16[1,64,12,128]{3,1,2,0:T(8,128)(2,1)}), bf16[1,3072,12,128]{3,1,2,0:T(8,128)(2,1)}) %all-gather.2.cloned.1.call-update) | async-done | bytes 9437200 | tf_op jit(solution)/shard_map/all_gather | solution.py:58
  155.7 12.7 %copy.35 = bf16[1,3072,12,128]{1,3,2,0:T(8,128)(2,1)} copy(bf16[1,3072,12,128]{3,1,2,0:T(8,128)(2,1)} %all-gather.2.cloned.1.call-done) | data formatting | bytes 18874368 | tf_op jit(solution)/shard_map/all_gather | solution.py:58
  168.4 6.7 %convolution_convert_fusion = bf16[96,1536]{1,0:T(8,128)(2,1)S(1)} fusion(bf16[3072,1536]{0,1:T(8,128)(2,1)} %bitcast.104, s32[96]{0:T(128)S(1)} %eq.85), kind=kOutput, calls=%fused_computation.63 | convolution fusion | flops 906412032 | bytes 9732480 | tf_op jit(solution)/shard_map/dot_general | solution.py:61
  184.3 7.8 %all-to-all-start = ((f32[48,3,256]{2,1,0:T(4,128)}), f32[48,3,256]{2,1,0:T(4,128)S(1)}, u32[]{:S(2)}, u32[]{:S(2)}) async-start(f32[48,3,256]{2,1,0:T(4,128)} %copy.41), calls=%async_computation | async-start | bytes 393216 | tf_op jit(solution)/shard_map/all_to_all | solution.py:142
  192.9 448.1 %while.14 = (s32[]{:T(128)}, f32[16,256]{1,0:T(8,128)}, f32[16,256]{1,0:T(8,128)S(1)}, f32[16,256]{1,0:T(8,128)S(1)}, f32[16,256]{1,0:T(8,128)S(1)}, /*index=5*/...) while((s32[]{:T(128)}, f32[16,256]{1,0:T(8,128)}, ...), condition=%wide.region_1.2_spmd, body=%wide.region_0.1_spmd.sunk | while | flops 418818 | bytes 765617 | solution.py:127
  193.6 3.4 collective-permute-start
  203.1 7.1 %collective-permute-start.3 = (f32[18,1]{1,0:T(8,128)S(1)}, f32[18,1]{1,0:T(8,128)S(1)}, u32[]{:S(2)}, u32[]{:S(2)}) collective-permute-start(f32[18,1]{1,0:T(8,128)S(1)} %get-tuple-element.208), channel_id=1, source_target_pairs={{8,0},{16,8},{24,16},{32,24},{40,32},{48,40},{56,48},{64,56},{72,6... | collective-permute-start | bytes 224 | tf_op jit(solution)/shard_map/while/body/eval_jaxpr/ppermute | solution.py:25
  211.7 4.1 collective-permute-start.4
  217.8 4.8 collective-permute-done.5
  224.5 7.5 %collective-permute-start.7 = (f32[2,18,1]{2,1,0:T(8,128)S(1)}, f32[2,18,1]{2,1,0:T(8,128)S(1)}, u32[]{:S(2)}, u32[]{:S(2)}) collective-permute-start(f32[2,18,1]{2,1,0:T(8,128)S(1)} %get-tuple-element.214), channel_id=1, source_target_pairs={{8,0},{16,8},{24,16},{32,24},{40,32},{48,40},{56,48},{64,56},{72,6... | collective-permute-start | bytes 440 | tf_op jit(solution)/shard_map/while/body/eval_jaxpr/ppermute | solution.py:25
  234.1 7.0 %collective-permute-done.2 = f32[18,1]{1,0:T(8,128)S(1)} collective-permute-done((f32[18,1]{1,0:T(8,128)}, f32[18,1]{1,0:T(8,128)S(1)}, u32[]{:S(2)}, u32[]{:S(2)}) %collective-permute-start.2) | collective-permute-done | bytes 104 | tf_op jit(solution)/shard_map/while/body/eval_jaxpr/ppermute | solution.py:24
  243.4 3.9 collective-permute-start
  249.3 3.5 collective-permute-done.1
  255.4 3.7 collective-permute-done.3
  269.8 7.2 %collective-permute-start.7 = (f32[2,18,1]{2,1,0:T(8,128)S(1)}, f32[2,18,1]{2,1,0:T(8,128)S(1)}, u32[]{:S(2)}, u32[]{:S(2)}) collective-permute-start(f32[2,18,1]{2,1,0:T(8,128)S(1)} %get-tuple-element.214), channel_id=1, source_target_pairs={{8,0},{16,8},{24,16},{32,24},{40,32},{48,40},{56,48},{64,56},{72,6... | collective-permute-start | bytes 440 | tf_op jit(solution)/shard_map/while/body/eval_jaxpr/ppermute | solution.py:25
  279.1 7.0 %collective-permute-done.2 = f32[18,1]{1,0:T(8,128)S(1)} collective-permute-done((f32[18,1]{1,0:T(8,128)}, f32[18,1]{1,0:T(8,128)S(1)}, u32[]{:S(2)}, u32[]{:S(2)}) %collective-permute-start.2) | collective-permute-done | bytes 104 | tf_op jit(solution)/shard_map/while/body/eval_jaxpr/ppermute | solution.py:24
  299.5 3.7 collective-permute-done.3
  303.3 3.1 collective-permute-start.4
  313.9 7.2 %collective-permute-start.7 = (f32[2,18,1]{2,1,0:T(8,128)S(1)}, f32[2,18,1]{2,1,0:T(8,128)S(1)}, u32[]{:S(2)}, u32[]{:S(2)}) collective-permute-start(f32[2,18,1]{2,1,0:T(8,128)S(1)} %get-tuple-element.214), channel_id=1, source_target_pairs={{8,0},{16,8},{24,16},{32,24},{40,32},{48,40},{56,48},{64,56},{72,6... | collective-permute-start | bytes 440 | tf_op jit(solution)/shard_map/while/body/eval_jaxpr/ppermute | solution.py:25
  323.3 7.0 %collective-permute-done.2 = f32[18,1]{1,0:T(8,128)S(1)} collective-permute-done((f32[18,1]{1,0:T(8,128)}, f32[18,1]{1,0:T(8,128)S(1)}, u32[]{:S(2)}, u32[]{:S(2)}) %collective-permute-start.2) | collective-permute-done | bytes 104 | tf_op jit(solution)/shard_map/while/body/eval_jaxpr/ppermute | solution.py:24
  343.7 3.7 collective-permute-done.3
  347.5 3.1 collective-permute-start.4
  358.1 7.2 %collective-permute-start.7 = (f32[2,18,1]{2,1,0:T(8,128)S(1)}, f32[2,18,1]{2,1,0:T(8,128)S(1)}, u32[]{:S(2)}, u32[]{:S(2)}) collective-permute-start(f32[2,18,1]{2,1,0:T(8,128)S(1)} %get-tuple-element.214), channel_id=1, source_target_pairs={{8,0},{16,8},{24,16},{32,24},{40,32},{48,40},{56,48},{64,56},{72,6... | collective-permute-start | bytes 440 | tf_op jit(solution)/shard_map/while/body/eval_jaxpr/ppermute | solution.py:25
  367.4 7.0 %collective-permute-done.2 = f32[18,1]{1,0:T(8,128)S(1)} collective-permute-done((f32[18,1]{1,0:T(8,128)}, f32[18,1]{1,0:T(8,128)S(1)}, u32[]{:S(2)}, u32[]{:S(2)}) %collective-permute-start.2) | collective-permute-done | bytes 104 | tf_op jit(solution)/shard_map/while/body/eval_jaxpr/ppermute | solution.py:24
  387.9 3.7 collective-permute-done.3
  402.3 7.2 %collective-permute-start.7 = (f32[2,18,1]{2,1,0:T(8,128)S(1)}, f32[2,18,1]{2,1,0:T(8,128)S(1)}, u32[]{:S(2)}, u32[]{:S(2)}) collective-permute-start(f32[2,18,1]{2,1,0:T(8,128)S(1)} %get-tuple-element.214), channel_id=1, source_target_pairs={{8,0},{16,8},{24,16},{32,24},{40,32},{48,40},{56,48},{64,56},{72,6... | collective-permute-start | bytes 440 | tf_op jit(solution)/shard_map/while/body/eval_jaxpr/ppermute | solution.py:25
  411.6 7.0 %collective-permute-done.2 = f32[18,1]{1,0:T(8,128)S(1)} collective-permute-done((f32[18,1]{1,0:T(8,128)}, f32[18,1]{1,0:T(8,128)S(1)}, u32[]{:S(2)}, u32[]{:S(2)}) %collective-permute-start.2) | collective-permute-done | bytes 104 | tf_op jit(solution)/shard_map/while/body/eval_jaxpr/ppermute | solution.py:24
  432.1 3.7 collective-permute-done.3
  435.8 3.1 collective-permute-start.4
  446.5 7.2 %collective-permute-start.7 = (f32[2,18,1]{2,1,0:T(8,128)S(1)}, f32[2,18,1]{2,1,0:T(8,128)S(1)}, u32[]{:S(2)}, u32[]{:S(2)}) collective-permute-start(f32[2,18,1]{2,1,0:T(8,128)S(1)} %get-tuple-element.214), channel_id=1, source_target_pairs={{8,0},{16,8},{24,16},{32,24},{40,32},{48,40},{56,48},{64,56},{72,6... | collective-permute-start | bytes 440 | tf_op jit(solution)/shard_map/while/body/eval_jaxpr/ppermute | solution.py:25
  455.8 7.0 %collective-permute-done.2 = f32[18,1]{1,0:T(8,128)S(1)} collective-permute-done((f32[18,1]{1,0:T(8,128)}, f32[18,1]{1,0:T(8,128)S(1)}, u32[]{:S(2)}, u32[]{:S(2)}) %collective-permute-start.2) | collective-permute-done | bytes 104 | tf_op jit(solution)/shard_map/while/body/eval_jaxpr/ppermute | solution.py:24
  476.2 3.7 collective-permute-done.3
  480.0 3.1 collective-permute-start.4
  490.6 7.2 %collective-permute-start.7 = (f32[2,18,1]{2,1,0:T(8,128)S(1)}, f32[2,18,1]{2,1,0:T(8,128)S(1)}, u32[]{:S(2)}, u32[]{:S(2)}) collective-permute-start(f32[2,18,1]{2,1,0:T(8,128)S(1)} %get-tuple-element.214), channel_id=1, source_target_pairs={{8,0},{16,8},{24,16},{32,24},{40,32},{48,40},{56,48},{64,56},{72,6... | collective-permute-start | bytes 440 | tf_op jit(solution)/shard_map/while/body/eval_jaxpr/ppermute | solution.py:25
  500.0 7.0 %collective-permute-done.2 = f32[18,1]{1,0:T(8,128)S(1)} collective-permute-done((f32[18,1]{1,0:T(8,128)}, f32[18,1]{1,0:T(8,128)S(1)}, u32[]{:S(2)}, u32[]{:S(2)}) %collective-permute-start.2) | collective-permute-done | bytes 104 | tf_op jit(solution)/shard_map/while/body/eval_jaxpr/ppermute | solution.py:24
  520.4 3.7 collective-permute-done.3
  534.8 7.2 %collective-permute-start.7 = (f32[2,18,1]{2,1,0:T(8,128)S(1)}, f32[2,18,1]{2,1,0:T(8,128)S(1)}, u32[]{:S(2)}, u32[]{:S(2)}) collective-permute-start(f32[2,18,1]{2,1,0:T(8,128)S(1)} %get-tuple-element.214), channel_id=1, source_target_pairs={{8,0},{16,8},{24,16},{32,24},{40,32},{48,40},{56,48},{64,56},{72,6... | collective-permute-start | bytes 440 | tf_op jit(solution)/shard_map/while/body/eval_jaxpr/ppermute | solution.py:25
  544.1 7.0 %collective-permute-done.2 = f32[18,1]{1,0:T(8,128)S(1)} collective-permute-done((f32[18,1]{1,0:T(8,128)}, f32[18,1]{1,0:T(8,128)S(1)}, u32[]{:S(2)}, u32[]{:S(2)}) %collective-permute-start.2) | collective-permute-done | bytes 104 | tf_op jit(solution)/shard_map/while/body/eval_jaxpr/ppermute | solution.py:24
  564.6 3.7 collective-permute-done.3
  579.0 7.2 %collective-permute-start.7 = (f32[2,18,1]{2,1,0:T(8,128)S(1)}, f32[2,18,1]{2,1,0:T(8,128)S(1)}, u32[]{:S(2)}, u32[]{:S(2)}) collective-permute-start(f32[2,18,1]{2,1,0:T(8,128)S(1)} %get-tuple-element.214), channel_id=1, source_target_pairs={{8,0},{16,8},{24,16},{32,24},{40,32},{48,40},{56,48},{64,56},{72,6... | collective-permute-start | bytes 440 | tf_op jit(solution)/shard_map/while/body/eval_jaxpr/ppermute | solution.py:25
  588.3 7.0 %collective-permute-done.2 = f32[18,1]{1,0:T(8,128)S(1)} collective-permute-done((f32[18,1]{1,0:T(8,128)}, f32[18,1]{1,0:T(8,128)S(1)}, u32[]{:S(2)}, u32[]{:S(2)}) %collective-permute-start.2) | collective-permute-done | bytes 104 | tf_op jit(solution)/shard_map/while/body/eval_jaxpr/ppermute | solution.py:24
  608.7 3.7 collective-permute-done.3
  623.1 7.2 %collective-permute-start.7 = (f32[2,18,1]{2,1,0:T(8,128)S(1)}, f32[2,18,1]{2,1,0:T(8,128)S(1)}, u32[]{:S(2)}, u32[]{:S(2)}) collective-permute-start(f32[2,18,1]{2,1,0:T(8,128)S(1)} %get-tuple-element.214), channel_id=1, source_target_pairs={{8,0},{16,8},{24,16},{32,24},{40,32},{48,40},{56,48},{64,56},{72,6... | collective-permute-start | bytes 440 | tf_op jit(solution)/shard_map/while/body/eval_jaxpr/ppermute | solution.py:25
  632.5 7.0 %collective-permute-done.2 = f32[18,1]{1,0:T(8,128)S(1)} collective-permute-done((f32[18,1]{1,0:T(8,128)}, f32[18,1]{1,0:T(8,128)S(1)}, u32[]{:S(2)}, u32[]{:S(2)}) %collective-permute-start.2) | collective-permute-done | bytes 104 | tf_op jit(solution)/shard_map/while/body/eval_jaxpr/ppermute | solution.py:24
  (342 shorter events, 254.3 us)
Async XLA Ops:
  7.2 148.5 %all-gather.2.cloned.1.call-start = ((), (), s32[]{:S(2)}) async-start(), calls=%async_computation.1 | async-start | bytes 9633792 | tf_op jit(solution)/shard_map/all_gather | solution.py:58
  8.8 18.6 %collective-permute-start.8 = (f32[1,256]{1,0:T(1,128)S(1)}, f32[1,256]{1,0:T(1,128)S(1)}, u32[]{:S(2)}, u32[]{:S(2)}) collective-permute-start(f32[1,256]{1,0:T(1,128)S(1)} %get-tuple-element.120), channel_id=1, source_target_pairs={{0,1},{1,2},{2,3},{3,4},{4,5},{5,6},{6,7},{7,384},{384,385},{385,3... | collective-permute-start | bytes 3080 | tf_op jit(solution)/shard_map/ppermute | solution.py:24
  12.3 15.1 %collective-permute-start.9 = (f32[1,256]{1,0:T(1,128)S(1)}, f32[1,256]{1,0:T(1,128)S(1)}, u32[]{:S(2)}, u32[]{:S(2)}) collective-permute-start(f32[1,256]{1,0:T(1,128)S(1)} %get-tuple-element.121), channel_id=1, source_target_pairs={{1,0},{2,1},{3,2},{4,3},{5,4},{6,5},{7,6},{384,7},{385,384},{386,3... | collective-permute-start | bytes 3080 | tf_op jit(solution)/shard_map/ppermute | solution.py:25
  27.5 11.3 %collective-permute-start.11 = (f32[18,1]{1,0:T(8,128)S(1)}, f32[18,1]{1,0:T(8,128)S(1)}, u32[]{:S(2)}, u32[]{:S(2)}) collective-permute-start(f32[18,1]{1,0:T(8,128)S(1)} %get-tuple-element.118), channel_id=1, source_target_pairs={{8,0},{16,8},{24,16},{32,24},{40,32},{48,40},{56,48},{64,56},{72,6... | collective-permute-start | bytes 224 | tf_op jit(solution)/shard_map/ppermute | solution.py:25
  36.9 8.9 %collective-permute-start.10 = (f32[18,1]{1,0:T(8,128)S(1)}, f32[18,1]{1,0:T(8,128)S(1)}, u32[]{:S(2)}, u32[]{:S(2)}) collective-permute-start(f32[18,1]{1,0:T(8,128)S(1)} %get-tuple-element.119), channel_id=1, source_target_pairs={{0,8},{8,16},{16,24},{24,32},{32,40},{40,48},{48,56},{56,64},{64,7... | collective-permute-start | bytes 224 | tf_op jit(solution)/shard_map/ppermute | solution.py:24
  184.3 458.0 %all-to-all-start = ((f32[48,3,256]{2,1,0:T(4,128)}), f32[48,3,256]{2,1,0:T(4,128)S(1)}, u32[]{:S(2)}, u32[]{:S(2)}) async-start(f32[48,3,256]{2,1,0:T(4,128)} %copy.41), calls=%async_computation | async-start | bytes 393216 | tf_op jit(solution)/shard_map/all_to_all | solution.py:142
  203.1 8.5 %collective-permute-start.3 = (f32[18,1]{1,0:T(8,128)S(1)}, f32[18,1]{1,0:T(8,128)S(1)}, u32[]{:S(2)}, u32[]{:S(2)}) collective-permute-start(f32[18,1]{1,0:T(8,128)S(1)} %get-tuple-element.208), channel_id=1, source_target_pairs={{8,0},{16,8},{24,16},{32,24},{40,32},{48,40},{56,48},{64,56},{72,6... | collective-permute-start | bytes 224 | tf_op jit(solution)/shard_map/while/body/eval_jaxpr/ppermute | solution.py:25
  211.7 6.0 collective-permute-start.4
  215.8 6.7 %collective-permute-start.5 = (f32[2,1,256]{2,1,0:T(1,128)S(1)}, f32[2,1,256]{2,1,0:T(1,128)S(1)}, u32[]{:S(2)}, u32[]{:S(2)}) collective-permute-start(f32[2,1,256]{2,1,0:T(1,128)S(1)} %get-tuple-element.212), channel_id=1, source_target_pairs={{1,0},{2,1},{3,2},{4,3},{5,4},{6,5},{7,6},{384,7},{385,384},{386,3... | collective-permute-start | bytes 6152 | tf_op jit(solution)/shard_map/while/body/eval_jaxpr/ppermute | solution.py:25
  222.6 11.4 %collective-permute-start.6 = (f32[2,18,1]{2,1,0:T(8,128)S(1)}, f32[2,18,1]{2,1,0:T(8,128)S(1)}, u32[]{:S(2)}, u32[]{:S(2)}) collective-permute-start(f32[2,18,1]{2,1,0:T(8,128)S(1)} %get-tuple-element.213), channel_id=1, source_target_pairs={{0,8},{8,16},{16,24},{24,32},{32,40},{40,48},{48,56},{56,64},{64,7... | collective-permute-start | bytes 440 | tf_op jit(solution)/shard_map/while/body/eval_jaxpr/ppermute | solution.py:24
  224.5 9.5 %collective-permute-start.7 = (f32[2,18,1]{2,1,0:T(8,128)S(1)}, f32[2,18,1]{2,1,0:T(8,128)S(1)}, u32[]{:S(2)}, u32[]{:S(2)}) collective-permute-start(f32[2,18,1]{2,1,0:T(8,128)S(1)} %get-tuple-element.214), channel_id=1, source_target_pairs={{8,0},{16,8},{24,16},{32,24},{40,32},{48,40},{56,48},{64,56},{72,6... | collective-permute-start | bytes 440 | tf_op jit(solution)/shard_map/while/body/eval_jaxpr/ppermute | solution.py:25
  232.1 9.1 %collective-permute-start.2 = (f32[18,1]{1,0:T(8,128)}, f32[18,1]{1,0:T(8,128)S(1)}, u32[]{:S(2)}, u32[]{:S(2)}) collective-permute-start(f32[18,1]{1,0:T(8,128)} %get-tuple-element.207), channel_id=1, source_target_pairs={{0,8},{8,16},{16,24},{24,32},{32,40},{40,48},{48,56},{56,64},{64,7... | collective-permute-start | bytes 224 | tf_op jit(solution)/shard_map/while/body/eval_jaxpr/ppermute | solution.py:24
  259.1 5.9 collective-permute-start.4
  267.9 11.1 %collective-permute-start.6 = (f32[2,18,1]{2,1,0:T(8,128)S(1)}, f32[2,18,1]{2,1,0:T(8,128)S(1)}, u32[]{:S(2)}, u32[]{:S(2)}) collective-permute-start(f32[2,18,1]{2,1,0:T(8,128)S(1)} %get-tuple-element.213), channel_id=1, source_target_pairs={{0,8},{8,16},{16,24},{24,32},{32,40},{40,48},{48,56},{56,64},{64,7... | collective-permute-start | bytes 440 | tf_op jit(solution)/shard_map/while/body/eval_jaxpr/ppermute | solution.py:24
  269.8 9.2 %collective-permute-start.7 = (f32[2,18,1]{2,1,0:T(8,128)S(1)}, f32[2,18,1]{2,1,0:T(8,128)S(1)}, u32[]{:S(2)}, u32[]{:S(2)}) collective-permute-start(f32[2,18,1]{2,1,0:T(8,128)S(1)} %get-tuple-element.214), channel_id=1, source_target_pairs={{8,0},{16,8},{24,16},{32,24},{40,32},{48,40},{56,48},{64,56},{72,6... | collective-permute-start | bytes 440 | tf_op jit(solution)/shard_map/while/body/eval_jaxpr/ppermute | solution.py:25
  277.0 9.1 %collective-permute-start.2 = (f32[18,1]{1,0:T(8,128)}, f32[18,1]{1,0:T(8,128)S(1)}, u32[]{:S(2)}, u32[]{:S(2)}) collective-permute-start(f32[18,1]{1,0:T(8,128)} %get-tuple-element.207), channel_id=1, source_target_pairs={{0,8},{8,16},{16,24},{24,32},{32,40},{40,48},{48,56},{56,64},{64,7... | collective-permute-start | bytes 224 | tf_op jit(solution)/shard_map/while/body/eval_jaxpr/ppermute | solution.py:24
  303.3 5.9 collective-permute-start.4
  312.0 11.1 %collective-permute-start.6 = (f32[2,18,1]{2,1,0:T(8,128)S(1)}, f32[2,18,1]{2,1,0:T(8,128)S(1)}, u32[]{:S(2)}, u32[]{:S(2)}) collective-permute-start(f32[2,18,1]{2,1,0:T(8,128)S(1)} %get-tuple-element.213), channel_id=1, source_target_pairs={{0,8},{8,16},{16,24},{24,32},{32,40},{40,48},{48,56},{56,64},{64,7... | collective-permute-start | bytes 440 | tf_op jit(solution)/shard_map/while/body/eval_jaxpr/ppermute | solution.py:24
  313.9 9.2 %collective-permute-start.7 = (f32[2,18,1]{2,1,0:T(8,128)S(1)}, f32[2,18,1]{2,1,0:T(8,128)S(1)}, u32[]{:S(2)}, u32[]{:S(2)}) collective-permute-start(f32[2,18,1]{2,1,0:T(8,128)S(1)} %get-tuple-element.214), channel_id=1, source_target_pairs={{8,0},{16,8},{24,16},{32,24},{40,32},{48,40},{56,48},{64,56},{72,6... | collective-permute-start | bytes 440 | tf_op jit(solution)/shard_map/while/body/eval_jaxpr/ppermute | solution.py:25
  321.2 9.1 %collective-permute-start.2 = (f32[18,1]{1,0:T(8,128)}, f32[18,1]{1,0:T(8,128)S(1)}, u32[]{:S(2)}, u32[]{:S(2)}) collective-permute-start(f32[18,1]{1,0:T(8,128)} %get-tuple-element.207), channel_id=1, source_target_pairs={{0,8},{8,16},{16,24},{24,32},{32,40},{40,48},{48,56},{56,64},{64,7... | collective-permute-start | bytes 224 | tf_op jit(solution)/shard_map/while/body/eval_jaxpr/ppermute | solution.py:24
  347.5 5.9 collective-permute-start.4
  356.2 11.1 %collective-permute-start.6 = (f32[2,18,1]{2,1,0:T(8,128)S(1)}, f32[2,18,1]{2,1,0:T(8,128)S(1)}, u32[]{:S(2)}, u32[]{:S(2)}) collective-permute-start(f32[2,18,1]{2,1,0:T(8,128)S(1)} %get-tuple-element.213), channel_id=1, source_target_pairs={{0,8},{8,16},{16,24},{24,32},{32,40},{40,48},{48,56},{56,64},{64,7... | collective-permute-start | bytes 440 | tf_op jit(solution)/shard_map/while/body/eval_jaxpr/ppermute | solution.py:24
  358.1 9.2 %collective-permute-start.7 = (f32[2,18,1]{2,1,0:T(8,128)S(1)}, f32[2,18,1]{2,1,0:T(8,128)S(1)}, u32[]{:S(2)}, u32[]{:S(2)}) collective-permute-start(f32[2,18,1]{2,1,0:T(8,128)S(1)} %get-tuple-element.214), channel_id=1, source_target_pairs={{8,0},{16,8},{24,16},{32,24},{40,32},{48,40},{56,48},{64,56},{72,6... | collective-permute-start | bytes 440 | tf_op jit(solution)/shard_map/while/body/eval_jaxpr/ppermute | solution.py:25
  365.4 9.1 %collective-permute-start.2 = (f32[18,1]{1,0:T(8,128)}, f32[18,1]{1,0:T(8,128)S(1)}, u32[]{:S(2)}, u32[]{:S(2)}) collective-permute-start(f32[18,1]{1,0:T(8,128)} %get-tuple-element.207), channel_id=1, source_target_pairs={{0,8},{8,16},{16,24},{24,32},{32,40},{40,48},{48,56},{56,64},{64,7... | collective-permute-start | bytes 224 | tf_op jit(solution)/shard_map/while/body/eval_jaxpr/ppermute | solution.py:24
  391.6 5.9 collective-permute-start.4
  400.4 11.1 %collective-permute-start.6 = (f32[2,18,1]{2,1,0:T(8,128)S(1)}, f32[2,18,1]{2,1,0:T(8,128)S(1)}, u32[]{:S(2)}, u32[]{:S(2)}) collective-permute-start(f32[2,18,1]{2,1,0:T(8,128)S(1)} %get-tuple-element.213), channel_id=1, source_target_pairs={{0,8},{8,16},{16,24},{24,32},{32,40},{40,48},{48,56},{56,64},{64,7... | collective-permute-start | bytes 440 | tf_op jit(solution)/shard_map/while/body/eval_jaxpr/ppermute | solution.py:24
  402.3 9.2 %collective-permute-start.7 = (f32[2,18,1]{2,1,0:T(8,128)S(1)}, f32[2,18,1]{2,1,0:T(8,128)S(1)}, u32[]{:S(2)}, u32[]{:S(2)}) collective-permute-start(f32[2,18,1]{2,1,0:T(8,128)S(1)} %get-tuple-element.214), channel_id=1, source_target_pairs={{8,0},{16,8},{24,16},{32,24},{40,32},{48,40},{56,48},{64,56},{72,6... | collective-permute-start | bytes 440 | tf_op jit(solution)/shard_map/while/body/eval_jaxpr/ppermute | solution.py:25
  409.5 9.1 %collective-permute-start.2 = (f32[18,1]{1,0:T(8,128)}, f32[18,1]{1,0:T(8,128)S(1)}, u32[]{:S(2)}, u32[]{:S(2)}) collective-permute-start(f32[18,1]{1,0:T(8,128)} %get-tuple-element.207), channel_id=1, source_target_pairs={{0,8},{8,16},{16,24},{24,32},{32,40},{40,48},{48,56},{56,64},{64,7... | collective-permute-start | bytes 224 | tf_op jit(solution)/shard_map/while/body/eval_jaxpr/ppermute | solution.py:24
  435.8 5.9 collective-permute-start.4
  444.5 11.1 %collective-permute-start.6 = (f32[2,18,1]{2,1,0:T(8,128)S(1)}, f32[2,18,1]{2,1,0:T(8,128)S(1)}, u32[]{:S(2)}, u32[]{:S(2)}) collective-permute-start(f32[2,18,1]{2,1,0:T(8,128)S(1)} %get-tuple-element.213), channel_id=1, source_target_pairs={{0,8},{8,16},{16,24},{24,32},{32,40},{40,48},{48,56},{56,64},{64,7... | collective-permute-start | bytes 440 | tf_op jit(solution)/shard_map/while/body/eval_jaxpr/ppermute | solution.py:24
  446.5 9.2 %collective-permute-start.7 = (f32[2,18,1]{2,1,0:T(8,128)S(1)}, f32[2,18,1]{2,1,0:T(8,128)S(1)}, u32[]{:S(2)}, u32[]{:S(2)}) collective-permute-start(f32[2,18,1]{2,1,0:T(8,128)S(1)} %get-tuple-element.214), channel_id=1, source_target_pairs={{8,0},{16,8},{24,16},{32,24},{40,32},{48,40},{56,48},{64,56},{72,6... | collective-permute-start | bytes 440 | tf_op jit(solution)/shard_map/while/body/eval_jaxpr/ppermute | solution.py:25
  453.7 9.1 %collective-permute-start.2 = (f32[18,1]{1,0:T(8,128)}, f32[18,1]{1,0:T(8,128)S(1)}, u32[]{:S(2)}, u32[]{:S(2)}) collective-permute-start(f32[18,1]{1,0:T(8,128)} %get-tuple-element.207), channel_id=1, source_target_pairs={{0,8},{8,16},{16,24},{24,32},{32,40},{40,48},{48,56},{56,64},{64,7... | collective-permute-start | bytes 224 | tf_op jit(solution)/shard_map/while/body/eval_jaxpr/ppermute | solution.py:24
  480.0 5.9 collective-permute-start.4
  488.7 11.1 %collective-permute-start.6 = (f32[2,18,1]{2,1,0:T(8,128)S(1)}, f32[2,18,1]{2,1,0:T(8,128)S(1)}, u32[]{:S(2)}, u32[]{:S(2)}) collective-permute-start(f32[2,18,1]{2,1,0:T(8,128)S(1)} %get-tuple-element.213), channel_id=1, source_target_pairs={{0,8},{8,16},{16,24},{24,32},{32,40},{40,48},{48,56},{56,64},{64,7... | collective-permute-start | bytes 440 | tf_op jit(solution)/shard_map/while/body/eval_jaxpr/ppermute | solution.py:24
  490.6 9.2 %collective-permute-start.7 = (f32[2,18,1]{2,1,0:T(8,128)S(1)}, f32[2,18,1]{2,1,0:T(8,128)S(1)}, u32[]{:S(2)}, u32[]{:S(2)}) collective-permute-start(f32[2,18,1]{2,1,0:T(8,128)S(1)} %get-tuple-element.214), channel_id=1, source_target_pairs={{8,0},{16,8},{24,16},{32,24},{40,32},{48,40},{56,48},{64,56},{72,6... | collective-permute-start | bytes 440 | tf_op jit(solution)/shard_map/while/body/eval_jaxpr/ppermute | solution.py:25
  497.9 9.1 %collective-permute-start.2 = (f32[18,1]{1,0:T(8,128)}, f32[18,1]{1,0:T(8,128)S(1)}, u32[]{:S(2)}, u32[]{:S(2)}) collective-permute-start(f32[18,1]{1,0:T(8,128)} %get-tuple-element.207), channel_id=1, source_target_pairs={{0,8},{8,16},{16,24},{24,32},{32,40},{40,48},{48,56},{56,64},{64,7... | collective-permute-start | bytes 224 | tf_op jit(solution)/shard_map/while/body/eval_jaxpr/ppermute | solution.py:24
  524.2 5.9 collective-permute-start.4
  532.9 11.1 %collective-permute-start.6 = (f32[2,18,1]{2,1,0:T(8,128)S(1)}, f32[2,18,1]{2,1,0:T(8,128)S(1)}, u32[]{:S(2)}, u32[]{:S(2)}) collective-permute-start(f32[2,18,1]{2,1,0:T(8,128)S(1)} %get-tuple-element.213), channel_id=1, source_target_pairs={{0,8},{8,16},{16,24},{24,32},{32,40},{40,48},{48,56},{56,64},{64,7... | collective-permute-start | bytes 440 | tf_op jit(solution)/shard_map/while/body/eval_jaxpr/ppermute | solution.py:24
  534.8 9.2 %collective-permute-start.7 = (f32[2,18,1]{2,1,0:T(8,128)S(1)}, f32[2,18,1]{2,1,0:T(8,128)S(1)}, u32[]{:S(2)}, u32[]{:S(2)}) collective-permute-start(f32[2,18,1]{2,1,0:T(8,128)S(1)} %get-tuple-element.214), channel_id=1, source_target_pairs={{8,0},{16,8},{24,16},{32,24},{40,32},{48,40},{56,48},{64,56},{72,6... | collective-permute-start | bytes 440 | tf_op jit(solution)/shard_map/while/body/eval_jaxpr/ppermute | solution.py:25
  542.0 9.1 %collective-permute-start.2 = (f32[18,1]{1,0:T(8,128)}, f32[18,1]{1,0:T(8,128)S(1)}, u32[]{:S(2)}, u32[]{:S(2)}) collective-permute-start(f32[18,1]{1,0:T(8,128)} %get-tuple-element.207), channel_id=1, source_target_pairs={{0,8},{8,16},{16,24},{24,32},{32,40},{40,48},{48,56},{56,64},{64,7... | collective-permute-start | bytes 224 | tf_op jit(solution)/shard_map/while/body/eval_jaxpr/ppermute | solution.py:24
  568.3 5.9 collective-permute-start.4
  577.0 11.1 %collective-permute-start.6 = (f32[2,18,1]{2,1,0:T(8,128)S(1)}, f32[2,18,1]{2,1,0:T(8,128)S(1)}, u32[]{:S(2)}, u32[]{:S(2)}) collective-permute-start(f32[2,18,1]{2,1,0:T(8,128)S(1)} %get-tuple-element.213), channel_id=1, source_target_pairs={{0,8},{8,16},{16,24},{24,32},{32,40},{40,48},{48,56},{56,64},{64,7... | collective-permute-start | bytes 440 | tf_op jit(solution)/shard_map/while/body/eval_jaxpr/ppermute | solution.py:24
  579.0 9.2 %collective-permute-start.7 = (f32[2,18,1]{2,1,0:T(8,128)S(1)}, f32[2,18,1]{2,1,0:T(8,128)S(1)}, u32[]{:S(2)}, u32[]{:S(2)}) collective-permute-start(f32[2,18,1]{2,1,0:T(8,128)S(1)} %get-tuple-element.214), channel_id=1, source_target_pairs={{8,0},{16,8},{24,16},{32,24},{40,32},{48,40},{56,48},{64,56},{72,6... | collective-permute-start | bytes 440 | tf_op jit(solution)/shard_map/while/body/eval_jaxpr/ppermute | solution.py:25
  586.2 9.1 %collective-permute-start.2 = (f32[18,1]{1,0:T(8,128)}, f32[18,1]{1,0:T(8,128)S(1)}, u32[]{:S(2)}, u32[]{:S(2)}) collective-permute-start(f32[18,1]{1,0:T(8,128)} %get-tuple-element.207), channel_id=1, source_target_pairs={{0,8},{8,16},{16,24},{24,32},{32,40},{40,48},{48,56},{56,64},{64,7... | collective-permute-start | bytes 224 | tf_op jit(solution)/shard_map/while/body/eval_jaxpr/ppermute | solution.py:24
  612.5 5.9 collective-permute-start.4
  621.2 11.1 %collective-permute-start.6 = (f32[2,18,1]{2,1,0:T(8,128)S(1)}, f32[2,18,1]{2,1,0:T(8,128)S(1)}, u32[]{:S(2)}, u32[]{:S(2)}) collective-permute-start(f32[2,18,1]{2,1,0:T(8,128)S(1)} %get-tuple-element.213), channel_id=1, source_target_pairs={{0,8},{8,16},{16,24},{24,32},{32,40},{40,48},{48,56},{56,64},{64,7... | collective-permute-start | bytes 440 | tf_op jit(solution)/shard_map/while/body/eval_jaxpr/ppermute | solution.py:24
  623.1 9.2 %collective-permute-start.7 = (f32[2,18,1]{2,1,0:T(8,128)S(1)}, f32[2,18,1]{2,1,0:T(8,128)S(1)}, u32[]{:S(2)}, u32[]{:S(2)}) collective-permute-start(f32[2,18,1]{2,1,0:T(8,128)S(1)} %get-tuple-element.214), channel_id=1, source_target_pairs={{8,0},{16,8},{24,16},{32,24},{40,32},{48,40},{56,48},{64,56},{72,6... | collective-permute-start | bytes 440 | tf_op jit(solution)/shard_map/while/body/eval_jaxpr/ppermute | solution.py:25
  630.4 9.1 %collective-permute-start.2 = (f32[18,1]{1,0:T(8,128)}, f32[18,1]{1,0:T(8,128)S(1)}, u32[]{:S(2)}, u32[]{:S(2)}) collective-permute-start(f32[18,1]{1,0:T(8,128)} %get-tuple-element.207), channel_id=1, source_target_pairs={{0,8},{8,16},{16,24},{24,32},{32,40},{40,48},{48,56},{56,64},{64,7... | collective-permute-start | bytes 224 | tf_op jit(solution)/shard_map/while/body/eval_jaxpr/ppermute | solution.py:24
  (72 other events, 711.8 us)
Sparse Core Ops, SparseCore 0:
  11.6 144.0 all-gather.1
where the time goes:
time: 656 us; the launch traced here: 652 us
  starting transfers between devices  285 us (43%)
  waiting for transfers between devices  280 us (43%)
  local copies, waits for them, and re-layouts  37.7 us (6%)
  other arithmetic  21.8 us (3%)
  between operations  14.2 us (2%)
  matrix products  12 us (2%)
    ppermute x42, starting transfers between devices, padded(): after = lax.ppermute(first, axis, down)  168 us
    all_gather x1, waiting for transfers between devices, shards(): shard_rows = lax.all_gather(atm_flux, 'blk', axis=1, tiled=True)  110 us
    ppermute x42, starting transfers between devices, padded(): before = lax.ppermute(last, axis, up)  108 us
    ppermute x42, waiting for transfers between devices, padded(): after = lax.ppermute(first, axis, down)  92.1 us
    ppermute x42, waiting for transfers between devices, padded(): before = lax.ppermute(last, axis, up)  77.4 us
    mul x10, other arithmetic, advance(): sea_cells * (eta - depth_step * (moving[0, 1:-1, 1:-1] - moving[0, 1:-1,...  14.8 us
  transfers between devices with their start and end apart: 86, of which 42 were waited for; matrix products, arithmetic and copies ran while one was open for 6% of the time, Pallas kernels for 0%

commit v1 on v0

v1 whole, which is shorter than its diff:
```python
import functools

import jax
import jax.numpy as jnp
from jax import lax
from jax.experimental import pallas as pl
from jax.experimental.pallas import tpu as pltpu
from jax.sharding import PartitionSpec as P

MESH = pl.DeviceIdType.MESH

SUBCYCLES = 10
FIELDS = 12
TILE = 128
KSRC = 3
CAP = 3
OY = 16
OX = 256
ATILES_DEV = 64
N_BLK = 48
N_ROW = 16
N_SUB = 8

EXT_Y = 40
EXT_X = 384

MSG = 16
ROWS = KSRC * OY * 8

drag_rate = 0.02
gravity_step = 0.6
depth_step = 0.6
force_step = 0.1
spread_rate = 0.1
filter_rate = 0.1

f32 = jnp.float32
bf16 = jnp.bfloat16
i32 = jnp.int32


def iota(shape, dim):
    return lax.broadcasted_iota(i32, shape, dim)


def pack_sides(fields):
    width = TILE // len(fields)
    lane = iota((OY, TILE), 1) // width
    first = last = jnp.zeros((OY, TILE), f32)
    for i, field in enumerate(fields):
        head, tail = field[:, :TILE], field[:, OX - TILE :]
        if i:
            head = pltpu.roll(head, i * width, 1)
        if i + 1 < len(fields):
            tail = pltpu.roll(tail, (i + 1) * width, 1)
        first = jnp.where(lane == i, head, first)
        last = jnp.where(lane == i, tail, last)
    return first, last


def extend(own, north, south, sides, i, count):
    width = TILE // count
    lane = iota((OY, TILE), 1)

    def beside(slot):
        east, west = sides[slot], sides[3 + slot]
        if i:
            east = pltpu.roll(east, TILE - i * width, 1)
        if i + 1 < count:
            west = pltpu.roll(west, TILE - (i + 1) * width, 1)
        return jnp.where(lane < TILE // 2, east, west)

    own = jnp.concatenate([own, beside(0)], axis=1)
    north = jnp.concatenate([north, beside(1)], axis=1)
    south = jnp.concatenate([south, beside(2)], axis=1)
    between = jnp.where(iota((8, EXT_X), 0) < 4, north[8:], south[:8])
    return jnp.concatenate([own, north[:8], between, south[8:]], axis=0)


def kernel(
    state_h, temp_h, land_h, flux_h, w_h, src_s, send_s, mix_s,
    ocean_o, atm_o,
    w_v, flux_v, temp_v, land_v, own, fown,
    listing, stage, send1, recv1, send2, recv2,
    packs, fpacks, rows_in, frows_in, sides_in, fsides_in,
    idcol, pick, back, listed, lhs, fscr, rscr, cscr,
    load_sem, tile_send, tile_recv, back_send, back_recv,
    halo_send, halo_recv, fhalo_send, fhalo_recv,
):
    comp = lax.axis_index("comp")
    blk = lax.axis_index("blk")
    sub = lax.axis_index("sub")
    row = comp * N_SUB + sub

    loads = [
        pltpu.make_async_copy(src, dst, load_sem.at[i])
        for i, (src, dst) in enumerate(
            [(flux_h, flux_v), (state_h, own.at[pl.ds(0, 3)]), (land_h, land_v), (temp_h, temp_v), (w_h, w_v)]
        )
    ]
    for load in loads:
        load.start()

    def device(dx, dy):
        to_row = lax.rem(row + dy + N_ROW, N_ROW)
        return (to_row // N_SUB, lax.rem(blk + dx + N_BLK, N_BLK), lax.rem(to_row, N_SUB))

    def partner(i):
        return (comp, lax.rem(blk + i, N_BLK), sub)

    barrier = pltpu.get_barrier_semaphore()

    def greet(i, carry):
        pl.semaphore_signal(barrier, inc=1, device_id=partner(i), device_id_type=MESH)
        return carry

    lax.fori_loop(1, N_BLK, greet, 0)
    for dx, dy in ((0, 1), (0, -1), (1, 1), (1, -1), (-1, 1), (-1, -1)):
        pl.semaphore_signal(barrier, inc=1, device_id=device(dx, dy), device_id_type=MESH)

    loads[0].wait()
    mixes = []
    for q in range(3):
        total = jnp.zeros((ATILES_DEV, TILE), f32)
        for f in range(FIELDS):
            total = total + mix_s[q, f] * flux_v[f].astype(f32)
        mixes.append(total)
    high = mixes[2].astype(bf16)
    rest = (mixes[2] - high.astype(f32)).astype(bf16)
    mixed = jnp.concatenate([mixes[0].astype(bf16), mixes[1].astype(bf16), high, rest], axis=0)

    upper = iota((8, TILE), 0) < 4
    for j in range(N_BLK):
        listing[pl.ds(j * MSG, 8), :] = jnp.where(upper, send_s[0, 0, 0, j], send_s[0, 1, 0, j])
        listing[pl.ds(j * MSG + 8, 8), :] = jnp.where(upper, send_s[0, 2, 0, j], -1)
    wanted = listing[...]
    wanted = jnp.where(wanted >= 0, wanted + iota((N_BLK * MSG, TILE), 0) % 4 * ATILES_DEV, -1)
    for c in range(2):
        stage[:, c * TILE : (c + 1) * TILE] = jnp.where(
            wanted == iota((N_BLK * MSG, TILE), 1) + c * TILE, 1.0, 0.0
        ).astype(bf16)
    send1[...] = (
        jnp.dot(stage[...], mixed, preferred_element_type=f32).astype(bf16).reshape(N_BLK, MSG, TILE)
    )

    loads[1].wait()
    loads[2].wait()
    own[3] = land_v[...].astype(f32)
    packs[0], packs[1] = pack_sides([own[i] for i in range(4)])

    pl.semaphore_wait(barrier, N_BLK - 1 + 6)

    def tile_copy(i, src, dst, send_sem, recv_sem):
        to = lax.rem(blk + i, N_BLK)
        return pltpu.make_async_remote_copy(
            src_ref=src.at[to], dst_ref=dst.at[blk], send_sem=send_sem, recv_sem=recv_sem,
            device_id=partner(i), device_id_type=MESH,
        )

    def send_tile(i, carry):
        tile_copy(i, send1, recv1, tile_send, tile_recv).start()
        return carry

    lax.fori_loop(1, N_BLK, send_tile, 0)

    def halo_copies(block, pair, rows_to, sides_to, send_sem, recv_sem):
        out = []

        def add(src, dst, dx, dy):
            i = len(out)
            out.append(
                pltpu.make_async_remote_copy(
                    src_ref=src, dst_ref=dst, send_sem=send_sem.at[i], recv_sem=recv_sem.at[i],
                    device_id=device(dx, dy), device_id_type=MESH,
                )
            )

        add(block, rows_to.at[0], 0, -1)
        add(block, rows_to.at[1], 0, 1)
        for slot, dy in ((0, 0), (1, -1), (2, 1)):
            add(pair.at[0], sides_to.at[slot], -1, dy)
            add(pair.at[1], sides_to.at[3 + slot], 1, dy)
        return out

    halo = halo_copies(own, packs, rows_in, sides_in, halo_send, halo_recv)
    for copy in halo:
        copy.start()
    recv1[blk] = send1[blk]

    lane = iota((8, TILE), 1)
    line = jnp.full((1, TILE), -1, i32)
    wide = [jnp.full((1, TILE), -1, i32) for _ in range(2)]
    lane1 = iota((1, TILE), 1)
    for k in range(KSRC):
        for y in range(OY):
            left, right = src_s[k, 0, y], src_s[k, 1, y]
            idcol[pl.ds((k * OY + y) * 8, 8), :] = jnp.where(upper, left, right)
            for n, value in enumerate((left, right)):
                place = (k * OY + y) * 2 + n
                line = jnp.where(lane1 == place, value, line)
                half, start = divmod(place * 2, TILE)
                wide[half] = jnp.where(lane1 // 2 == start // 2, value, wide[half])
    ids = idcol[...]
    spot = iota((ROWS, TILE), 0) // 4
    at = iota((ROWS, TILE), 1)
    again = jnp.max(jnp.where((ids == line) & (spot < at), 1, 0), axis=0, keepdims=True)
    owners = ids // ATILES_DEV
    lower = (line // ATILES_DEV == owners) & (line < ids) & (again == 0) & (line >= 0)
    rank = jnp.dot(
        jnp.where(lower, 1.0, 0.0).astype(bf16), jnp.ones((TILE, TILE), bf16), preferred_element_type=f32
    ).astype(i32)
    target = owners * MSG + rank * 4 + iota((ROWS, TILE), 0) % 4
    for c in range(N_BLK * MSG // TILE):
        pick[:, c * TILE : (c + 1) * TILE] = jnp.where(target == at + c * TILE, 1.0, 0.0).astype(bf16)
    for c in range(2):
        mine = jnp.where(spot == (at + c * TILE) // 2, jnp.where(iota((ROWS, TILE), 0) % 4 == 0, rank, 0), 0)
        rank_line = jnp.sum(mine, axis=0, keepdims=True)
        to = (wide[c] // ATILES_DEV) * 8 + rank_line * 2 + lane1 % 2
        to = jnp.where(wide[c] >= 0, to, -1)
        back[:, c * TILE : (c + 1) * TILE] = jnp.where(to == iota((N_BLK * 8, TILE), 0), 1.0, 0.0).astype(bf16)
    for c in range(3):
        tile_line = jnp.full((1, TILE), -1, i32)
        for j in range(16):
            for s in range(CAP):
                tile_line = jnp.where(lane1 // 2 == j * 4 + s, send_s[0, s, 0, c * 16 + j], tile_line)
        tile_line = tile_line * 2 + lane1 % 2
        listed[:, c * TILE : (c + 1) * TILE] = jnp.where(
            tile_line == iota((2 * ATILES_DEV, TILE), 0), 1.0, 0.0
        ).astype(bf16)
    rscr[...] = jnp.zeros_like(rscr)

    others = pl.ds(0, N_BLK - 1)
    pltpu.make_async_copy(send1.at[others], recv1.at[others], tile_recv).wait()

    picked = jnp.dot(
        pick[...], recv1[...].reshape(N_BLK * MSG, TILE), preferred_element_type=f32
    ).astype(bf16)
    lhs[...] = jnp.concatenate([picked[k * TILE : (k + 1) * TILE] for k in range(KSRC)], axis=1)
    loads[4].wait()

    def weights(y):
        return jnp.concatenate([w_v[y, n].reshape(KSRC * TILE, TILE) for n in range(2)], axis=1)

    for y in range(OY):
        out = jnp.dot(lhs[pl.ds(y // 2 * 16, 16), :], weights(y), preferred_element_type=f32)
        for n in range(2):
            fscr[pl.ds(n * TILE + y * 8, 8), :] = out[y % 2 * 8 : y % 2 * 8 + 8, n * TILE : (n + 1) * TILE]

    def forcing(q):
        return jnp.concatenate(
            [fscr[pl.ds(n * TILE + 4 * n + q, OY, stride=8), :] for n in range(2)], axis=1
        )

    fown[0], fown[1] = forcing(0), forcing(1)
    fpacks[0], fpacks[1] = pack_sides([fown[0], fown[1]])
    fhalo = halo_copies(fown, fpacks, frows_in, fsides_in, fhalo_send, fhalo_recv)
    for copy in fhalo:
        copy.start()

    loads[3].wait()
    sea = own[3]
    surface = sea * (temp_v[...] + (forcing(2) + forcing(3)))
    ice = sea * jax.nn.sigmoid(-2.0 * (surface + 1.0))
    for f, field in enumerate((surface, ice)):
        field = field.astype(bf16).astype(f32)
        for n in range(2):
            rscr[pl.ds(n * 4 * OY + 2 * n + f, OY, stride=4), :] = field[:, n * TILE : (n + 1) * TILE]
    returned = jnp.concatenate([rscr[: 4 * OY], rscr[4 * OY :]], axis=1).astype(bf16)
    for y in range(OY):
        out = lax.dot_general(
            returned[y // 4 * 16 : y // 4 * 16 + 16], weights(y), (((1,), (1,)), ((), ())),
            preferred_element_type=f32,
        )
        cscr[pl.ds(y * 4, 4), :] = out[y % 4 * 4 : y % 4 * 4 + 4]
    terms = jnp.concatenate([cscr[:, k * TILE : (k + 1) * TILE] for k in range(KSRC)], axis=0)

    def routed(table, rows):
        top = rows.astype(bf16)
        rest = (rows - top.astype(f32)).astype(bf16)
        return jnp.dot(table, top, preferred_element_type=f32) + jnp.dot(table, rest, preferred_element_type=f32)

    send2[...] = routed(back[:, : 4 * OY * KSRC], terms).reshape(N_BLK, 8, TILE)

    def send_back(i, carry):
        tile_copy(i, send2, recv2, back_send, back_recv).start()
        return carry

    lax.fori_loop(1, N_BLK, send_back, 0)
    recv2[blk] = send2[blk]

    for copy in halo:
        copy.wait_recv()
    around = [
        extend(own[i], rows_in[0, i], rows_in[1, i], [sides_in[j] for j in range(6)], i, 4) for i in range(4)
    ]
    eta, east, north, sea = around
    east_open = sea * pltpu.roll(sea, EXT_X - 1, 1)
    north_open = sea * pltpu.roll(sea, EXT_Y - 1, 0)

    for copy in fhalo:
        copy.wait_recv()
    push = [
        extend(fown[i], frows_in[0, i], frows_in[1, i], [fsides_in[j] for j in range(6)], i, 2) for i in range(2)
    ]
    push_east = force_step * east_open * push[0]
    push_north = force_step * north_open * push[1]

    def from_east(x):
        return pltpu.roll(x, EXT_X - 1, 1)

    def from_west(x):
        return pltpu.roll(x, 1, 1)

    def from_north(x):
        return pltpu.roll(x, EXT_Y - 1, 0)

    def from_south(x):
        return pltpu.roll(x, 1, 0)

    def advance(_, carried):
        eta, east, north = carried
        slope_east = east_open * (from_east(eta) - eta)
        slope_north = north_open * (from_north(eta) - eta)
        east = (1.0 - drag_rate) * east_open * east - gravity_step * slope_east + push_east
        north = (1.0 - drag_rate) * north_open * north - gravity_step * slope_north + push_north
        flow_east = depth_step * east - spread_rate * slope_east
        flow_north = depth_step * north - spread_rate * slope_north
        eta = sea * (eta - (flow_east - from_west(flow_east)) - (flow_north - from_south(flow_north)))

        def smooth(x):
            around = from_east(x) + from_west(x) + from_north(x) + from_south(x)
            return (1.0 - 4.0 * filter_rate) * x + filter_rate * around

        return eta, east_open * smooth(east), north_open * smooth(north)

    final = lax.fori_loop(0, SUBCYCLES, advance, (eta, east, north))
    for i in range(3):
        ocean_o[i] = final[i][:OY, :OX]

    pltpu.make_async_copy(send2.at[others], recv2.at[others], back_recv).wait()
    atm_o[...] = routed(listed[...], recv2[...].reshape(N_BLK * 8, TILE))

    pltpu.make_async_copy(send1.at[others], recv1.at[others], tile_send).wait()
    pltpu.make_async_copy(send2.at[others], recv2.at[others], back_send).wait()
    for copy in halo + fhalo:
        copy.wait_send()


def shards(ocean_state, sea_temp, land_mask, atm_flux, remap_w, source_tile, send_tiles, flux_mix):
    hbm = pl.BlockSpec(memory_space=pl.ANY)
    smem = pl.BlockSpec(memory_space=pltpu.SMEM)
    vmem = pl.BlockSpec(memory_space=pltpu.VMEM)
    ocean, atm = pl.pallas_call(
        kernel,
        out_shape=(
            jax.ShapeDtypeStruct((3, OY, OX), f32),
            jax.ShapeDtypeStruct((2 * ATILES_DEV, TILE), f32),
        ),
        in_specs=[hbm] * 5 + [smem] * 3,
        out_specs=(vmem, vmem),
        scratch_shapes=[
            pltpu.VMEM((OY, 2, KSRC, TILE, TILE), bf16),
            pltpu.VMEM((FIELDS, ATILES_DEV, TILE), bf16),
            pltpu.VMEM((OY, OX), f32),
            pltpu.VMEM((OY, OX), i32),
            pltpu.VMEM((4, OY, OX), f32),
            pltpu.VMEM((2, OY, OX), f32),
            pltpu.VMEM((N_BLK * MSG, TILE), i32),
            pltpu.VMEM((N_BLK * MSG, 4 * ATILES_DEV), bf16),
            pltpu.VMEM((N_BLK, MSG, TILE), bf16),
            pltpu.VMEM((N_BLK, MSG, TILE), bf16),
            pltpu.VMEM((N_BLK, 8, TILE), f32),
            pltpu.VMEM((N_BLK, 8, TILE), f32),
            pltpu.VMEM((2, OY, TILE), f32),
            pltpu.VMEM((2, OY, TILE), f32),
            pltpu.VMEM((2, 4, OY, OX), f32),
            pltpu.VMEM((2, 2, OY, OX), f32),
            pltpu.VMEM((6, OY, TILE), f32),
            pltpu.VMEM((6, OY, TILE), f32),
            pltpu.VMEM((ROWS, TILE), i32),
            pltpu.VMEM((ROWS, N_BLK * MSG), bf16),
            pltpu.VMEM((N_BLK * 8, 2 * TILE), bf16),
            pltpu.VMEM((2 * ATILES_DEV, N_BLK * 8), bf16),
            pltpu.VMEM((TILE, KSRC * TILE), bf16),
            pltpu.VMEM((2 * TILE, TILE), f32),
            pltpu.VMEM((8 * OY, TILE), f32),
            pltpu.VMEM((4 * OY, KSRC * TILE), f32),
            pltpu.SemaphoreType.DMA((5,)),
            pltpu.SemaphoreType.DMA,
            pltpu.SemaphoreType.DMA,
            pltpu.SemaphoreType.DMA,
            pltpu.SemaphoreType.DMA,
            pltpu.SemaphoreType.DMA((8,)),
            pltpu.SemaphoreType.DMA((8,)),
            pltpu.SemaphoreType.DMA((8,)),
            pltpu.SemaphoreType.DMA((8,)),
        ],
        compiler_params=pltpu.CompilerParams(
            collective_id=0, has_side_effects=True, vmem_limit_bytes=60 * 1024 * 1024
        ),
    )(
        ocean_state, sea_temp, land_mask,
        jnp.transpose(atm_flux[0], (1, 0, 2)),
        remap_w,
        jnp.transpose(source_tile, (2, 1, 0)),
        jnp.transpose(send_tiles, (0, 3, 1, 2)),
        flux_mix,
    )
    return ocean, atm.reshape(1, ATILES_DEV, 2, TILE)


def solution(mesh):
    placed = (
        P(None, ("comp", "sub"), "blk"),
        P(("comp", "sub"), "blk"),
        P(("comp", "sub"), "blk"),
        P(("comp", "sub"), "blk", None, None),
        P(("comp", "sub"), "blk", None, None, None),
        P(("comp", "sub"), "blk", None),
        P(("comp", "sub"), "blk", None, None),
        P(),
    )
    return jax.shard_map(
        shards,
        mesh=mesh,
        in_specs=placed,
        out_specs=(P(None, ("comp", "sub"), "blk"), P(("comp", "sub"), "blk", None, None)),
        check_vma=False,
    )
```

time: 656 us -> 51.8 us (0.08)
  the two profiles are of different devices: /device:TPU:8 before, /device:TPU:1 now
where the time goes in v1:
time: 51.8 us; the launch traced here: 51.6 us
  Pallas kernels  48 us (93%)
  local copies, waits for them, and re-layouts  2.89 us (6%)
  between operations  0.64 us (1%)
    pallas_call x1, Pallas kernels, shards(): pl.pallas_call(kernel, out_shape=(jax.ShapeDtypeStruct((3, OY, OX), f32),...  48 us
    unnamed x2, local copies, waits for them, and re-layouts  2.89 us

profile of v1, /device:TPU:1, one launch (start us, length us, event | category | flops | bytes accessed | tf_op | source)
XLA Modules:
  0.0 51.6 jit_solution(7434669593635034377)
XLA Ops:
  0.6 48.0 %shard_map.95 = (f32[3,16,256]{2,1,0:T(8,128)}, f32[128,128]{1,0:T(8,128)}) custom-call(f32[3,16,256]{2,1,0:T(8,128)} %state_h.1, f32[16,256]{1,0:T(8,128)} %temp_h.1, s32[16,256]{1,0:T(8,128)} %land_h.1, bf16[12,64,128]{2,1,0:T(8,128)(2,1)} %bitcast.6, bf16[16,2,3,128,128]{4,3,2,1,0:T(8,128)(2,1)} %w_h.1, s32[3,2,16]{2,1,0:T(2,128)} %bitcast.8, ...), custom_call_target="tpu_custom_call" | custom-call | tf_op jit(solution)/shard_map/pallas_call | solution.py:353
  48.7 1.4 %copy.12 = f32[3,16,256]{2,1,0:T(8,128)} copy(f32[3,16,256]{2,1,0:T(8,128)} %get-tuple-element.8) | data formatting | bytes 98304
  50.1 1.5 %copy.13 = f32[1,64,2,128]{3,2,1,0:T(2,128)} copy(f32[1,64,2,128]{3,2,1,0:T(2,128)} %bitcast.7) | data formatting | bytes 131072

commit v2 on v1

v2 whole, which is shorter than its diff:
```python
import functools

import jax
import jax.numpy as jnp
from jax import lax
from jax.experimental import pallas as pl
from jax.experimental.pallas import tpu as pltpu
from jax.sharding import PartitionSpec as P

MESH = pl.DeviceIdType.MESH

SUBCYCLES = 10
FIELDS = 12
TILE = 128
KSRC = 3
CAP = 3
OY = 16
OX = 256
ATILES_DEV = 64
N_BLK = 48
N_ROW = 16
N_SUB = 8

EXT_Y = 40
EXT_X = 384

MSG = 8
REFS = KSRC * 2 * OY

drag_rate = 0.02
gravity_step = 0.6
depth_step = 0.6
force_step = 0.1
spread_rate = 0.1
filter_rate = 0.1

f32 = jnp.float32
bf16 = jnp.bfloat16
i32 = jnp.int32


def iota(shape, dim):
    return lax.broadcasted_iota(i32, shape, dim)


def pack_sides(fields):
    width = TILE // len(fields)
    lane = iota((OY, TILE), 1) // width
    first = last = jnp.zeros((OY, TILE), f32)
    for i, field in enumerate(fields):
        head, tail = field[:, :TILE], field[:, OX - TILE :]
        if i:
            head = pltpu.roll(head, i * width, 1)
        if i + 1 < len(fields):
            tail = pltpu.roll(tail, (i + 1) * width, 1)
        first = jnp.where(lane == i, head, first)
        last = jnp.where(lane == i, tail, last)
    return first, last


def extend(own, north, south, sides, i, count):
    width = TILE // count
    lane = iota((OY, TILE), 1)

    def beside(slot):
        east, west = sides[slot], sides[3 + slot]
        if i:
            east = pltpu.roll(east, TILE - i * width, 1)
        if i + 1 < count:
            west = pltpu.roll(west, TILE - (i + 1) * width, 1)
        return jnp.where(lane < TILE // 2, east, west)

    own = jnp.concatenate([own, beside(0)], axis=1)
    north = jnp.concatenate([north, beside(1)], axis=1)
    south = jnp.concatenate([south, beside(2)], axis=1)
    between = jnp.where(iota((8, EXT_X), 0) < 4, north[8:], south[:8])
    return jnp.concatenate([own, north[:8], between, south[8:]], axis=0)


def stage_tiles(flux_v, send_s, mix_s, listing, stage, send_a, send_b):
    mixes = []
    for q in range(3):
        total = jnp.zeros((ATILES_DEV, TILE), f32)
        for f in range(FIELDS):
            total = total + mix_s[q, f] * flux_v[f].astype(f32)
        mixes.append(total)
    high = mixes[2].astype(bf16)
    rest = (mixes[2] - high.astype(f32)).astype(bf16)

    line = iota((8, TILE), 0)
    takes = [(line == s) | (line == s + CAP) for s in range(CAP)]
    for j in range(N_BLK):
        tiles = jnp.full((8, TILE), -1, i32)
        for s in range(CAP):
            tiles = jnp.where(takes[s], send_s[0, s, 0, j], tiles)
        listing[pl.ds(j * MSG, MSG), :] = tiles
    wanted = listing[...]
    second = iota((N_BLK * MSG, TILE), 0) % MSG >= CAP
    wanted = jnp.where(wanted >= 0, wanted + jnp.where(second, ATILES_DEV, 0), -1)
    stage[...] = jnp.where(wanted == iota((N_BLK * MSG, TILE), 1), 1.0, 0.0).astype(bf16)
    for parts, send in (((high, rest), send_a), ((mixes[0].astype(bf16), mixes[1].astype(bf16)), send_b)):
        rows = jnp.dot(stage[...], jnp.concatenate(parts, axis=0), preferred_element_type=f32)
        send[...] = rows.astype(bf16).reshape(N_BLK, MSG, TILE)


def tables(src_s, send_s, idcol, pick, back, listed):
    line = iota((8, TILE), 0)
    refs = jnp.full((1, TILE), -1, i32)
    wide = [jnp.full((1, TILE), -1, i32) for _ in range(2)]
    lane1 = iota((1, TILE), 1)
    for k in range(KSRC):
        for n in range(2):
            for half in range(2):
                column = jnp.full((8, TILE), -1, i32)
                for i in range(8):
                    y = half * 8 + i
                    value = src_s[k, n, y]
                    place = (k * 2 + n) * OY + y
                    column = jnp.where(line == i, value, column)
                    refs = jnp.where(lane1 == place, value, refs)
                    pair = k * 32 + y * 2 + n
                    wide[pair // 64] = jnp.where(lane1 // 2 == pair % 64, value, wide[pair // 64])
                idcol[pl.ds((k * 2 + n) * OY + half * 8, 8), :] = column
    ids = idcol[...]
    spot = iota((REFS, TILE), 0)
    at = iota((REFS, TILE), 1)
    again = jnp.max(jnp.where((ids == refs) & (spot < at), 1, 0), axis=0, keepdims=True)
    owners = ids // ATILES_DEV
    lower = (refs // ATILES_DEV == owners) & (refs < ids) & (again == 0) & (refs >= 0)
    rank = jnp.dot(
        jnp.where(lower, 1.0, 0.0).astype(bf16), jnp.ones((TILE, TILE), bf16), preferred_element_type=f32
    ).astype(i32)
    target = owners * MSG + rank
    for c in range(N_BLK * MSG // TILE):
        for p in range(2):
            hit = jnp.where(target + p * CAP == at + c * TILE, 1.0, 0.0).astype(bf16)
            for k in range(KSRC):
                pick[pl.ds((k * 2 + p) * 32, 32), c * TILE : (c + 1) * TILE] = hit[k * 32 : (k + 1) * 32]
    order = spot // 32 * 32 + spot % OY * 2 + spot // OY % 2
    for c in range(2):
        rank_line = jnp.sum(jnp.where(order == at // 2 + c * 64, rank, 0), axis=0, keepdims=True)
        to = (wide[c] // ATILES_DEV) * MSG + rank_line * 2 + lane1 % 2
        to = jnp.where(wide[c] >= 0, to, -1)
        back[:, c * TILE : (c + 1) * TILE] = jnp.where(to == iota((N_BLK * MSG, TILE), 0), 1.0, 0.0).astype(bf16)
    for c in range(3):
        tile_line = jnp.full((1, TILE), -1, i32)
        for j in range(16):
            for s in range(CAP):
                tile_line = jnp.where(lane1 // 2 == j * 4 + s, send_s[0, s, 0, c * 16 + j], tile_line)
        tile_line = tile_line * 2 + lane1 % 2
        listed[:, c * TILE : (c + 1) * TILE] = jnp.where(
            tile_line == iota((2 * ATILES_DEV, TILE), 0), 1.0, 0.0
        ).astype(bf16)


def weights(w_v, y):
    return jnp.concatenate([w_v[y, n].reshape(KSRC * TILE, TILE) for n in range(2)], axis=1)


def turn_weights(w_v, wt_v):
    for y in range(OY):
        wt_v[y] = weights(w_v, y).T


def remap(pick, recv, lhs, w_v):
    picked = jnp.dot(
        pick[...], recv[...].reshape(N_BLK * MSG, TILE), preferred_element_type=f32
    ).astype(bf16)
    lhs[...] = jnp.concatenate([picked[k * 64 : (k + 1) * 64] for k in range(KSRC)], axis=1)
    row = iota((OY, TILE), 0)
    parts = [[jnp.zeros((OY, TILE), f32) for _ in range(2)] for _ in range(2)]
    for y in range(OY):
        out = jnp.dot(lhs[...], weights(w_v, y), preferred_element_type=f32)
        for p in range(2):
            for n in range(2):
                rows = out[(p * 2 + n) * OY : (p * 2 + n + 1) * OY, n * TILE : (n + 1) * TILE]
                parts[p][n] = jnp.where(row == y, rows, parts[p][n])
    return [jnp.concatenate(part, axis=1) for part in parts]


def remap_back(sea, temp, push, wt_v, rscr, cscr, back, send2):
    surface = sea * (temp + push)
    ice = sea * jax.nn.sigmoid(-2.0 * (surface + 1.0))
    for f, field in enumerate((surface, ice)):
        field = field.astype(bf16).astype(f32)
        for n in range(2):
            rscr[pl.ds(n * 4 * OY + 2 * n + f, OY, stride=4), :] = field[:, n * TILE : (n + 1) * TILE]
    returned = jnp.concatenate([rscr[: 4 * OY], rscr[4 * OY :]], axis=1).astype(bf16)
    for y in range(OY):
        out = jnp.dot(returned[y // 4 * 16 : y // 4 * 16 + 16], wt_v[y], preferred_element_type=f32)
        cscr[pl.ds(y * 4, 4), :] = out[y % 4 * 4 : y % 4 * 4 + 4]
    terms = jnp.concatenate([cscr[:, k * TILE : (k + 1) * TILE] for k in range(KSRC)], axis=0)
    table = back[:, : 4 * OY * KSRC]
    top = terms.astype(bf16)
    rest = (terms - top.astype(f32)).astype(bf16)
    sums = jnp.dot(table, top, preferred_element_type=f32) + jnp.dot(table, rest, preferred_element_type=f32)
    send2[...] = sums.astype(bf16).reshape(N_BLK, MSG, TILE)


def gather_back(listed, recv2, atm_o):
    atm_o[...] = jnp.dot(listed[...], recv2[...].reshape(N_BLK * MSG, TILE), preferred_element_type=f32)


def subcycles(around, push, ocean_o):
    eta, east, north, sea = around
    east_open = sea * pltpu.roll(sea, EXT_X - 1, 1)
    north_open = sea * pltpu.roll(sea, EXT_Y - 1, 0)

    push_east = force_step * east_open * push[0]
    push_north = force_step * north_open * push[1]

    def from_east(x):
        return pltpu.roll(x, EXT_X - 1, 1)

    def from_west(x):
        return pltpu.roll(x, 1, 1)

    def from_north(x):
        return pltpu.roll(x, EXT_Y - 1, 0)

    def from_south(x):
        return pltpu.roll(x, 1, 0)

    def advance(_, carried):
        eta, east, north = carried
        slope_east = east_open * (from_east(eta) - eta)
        slope_north = north_open * (from_north(eta) - eta)
        east = (1.0 - drag_rate) * east_open * east - gravity_step * slope_east + push_east
        north = (1.0 - drag_rate) * north_open * north - gravity_step * slope_north + push_north
        flow_east = depth_step * east - spread_rate * slope_east
        flow_north = depth_step * north - spread_rate * slope_north
        eta = sea * (eta - (flow_east - from_west(flow_east)) - (flow_north - from_south(flow_north)))

        def smooth(x):
            around = from_east(x) + from_west(x) + from_north(x) + from_south(x)
            return (1.0 - 4.0 * filter_rate) * x + filter_rate * around

        return eta, east_open * smooth(east), north_open * smooth(north)

    final = lax.fori_loop(0, SUBCYCLES, advance, (eta, east, north))
    for i in range(3):
        ocean_o[i] = final[i][:OY, :OX]


def kernel(
    state_h, temp_h, land_h, flux_h, w_h, src_h, send_h, mix_h,
    ocean_o, atm_o,
    src_s, send_s, mix_s,
    w_v, wt_v, flux_v, temp_v, land_v, own, fown,
    listing, stage, send_a, recv_a, send_b, recv_b, send2, recv2,
    packs, fpacks, rows_in, frows_in, sides_in, fsides_in,
    idcol, pick, back, listed, lhs, rscr, cscr,
    load_sem, a_send, a_recv, b_send, b_recv, back_send, back_recv,
    halo_send, halo_recv, fhalo_send, fhalo_recv,
):
    comp = lax.axis_index("comp")
    blk = lax.axis_index("blk")
    sub = lax.axis_index("sub")
    row = comp * N_SUB + sub

    def device(dx, dy):
        to_row = lax.rem(row + dy + N_ROW, N_ROW)
        return (to_row // N_SUB, lax.rem(blk + dx + N_BLK, N_BLK), lax.rem(to_row, N_SUB))

    def partner(i):
        return (comp, lax.rem(blk + i, N_BLK), sub)

    loads = [
        pltpu.make_async_copy(src, dst, load_sem.at[i])
        for i, (src, dst) in enumerate(
            [
                (mix_h, mix_s), (flux_h, flux_v), (send_h, send_s), (src_h, src_s),
                (state_h, own.at[pl.ds(0, 3)]), (land_h, land_v), (temp_h, temp_v), (w_h, w_v),
            ]
        )
    ]
    for load in loads:
        load.start()

    barrier = pltpu.get_barrier_semaphore()

    def greet(i, carry):
        pl.semaphore_signal(barrier, inc=1, device_id=partner(i), device_id_type=MESH)
        return carry

    lax.fori_loop(1, N_BLK, greet, 0)
    for dx, dy in ((0, 1), (0, -1), (1, 1), (1, -1), (-1, 1), (-1, -1)):
        pl.semaphore_signal(barrier, inc=1, device_id=device(dx, dy), device_id_type=MESH)

    for load in loads[:3]:
        load.wait()
    stage_tiles(flux_v, send_s, mix_s, listing, stage, send_a, send_b)

    pl.semaphore_wait(barrier, N_BLK - 1 + 6)

    def send_all(src, dst, send_sem, recv_sem):
        def send(i, carry):
            pltpu.make_async_remote_copy(
                src_ref=src.at[lax.rem(blk + i, N_BLK)], dst_ref=dst.at[blk],
                send_sem=send_sem, recv_sem=recv_sem,
                device_id=partner(i), device_id_type=MESH,
            ).start()
            return carry

        lax.fori_loop(1, N_BLK, send, 0)

    others = pl.ds(0, N_BLK - 1)

    def all_of(src, dst, sem):
        return pltpu.make_async_copy(src.at[others], dst.at[others], sem)

    send_all(send_a, recv_a, a_send, a_recv)
    send_all(send_b, recv_b, b_send, b_recv)

    def halo_copies(block, pair, rows_to, sides_to, send_sem, recv_sem):
        out = []

        def add(src, dst, dx, dy):
            i = len(out)
            out.append(
                pltpu.make_async_remote_copy(
                    src_ref=src, dst_ref=dst, send_sem=send_sem.at[i], recv_sem=recv_sem.at[i],
                    device_id=device(dx, dy), device_id_type=MESH,
                )
            )

        add(block, rows_to.at[0], 0, -1)
        add(block, rows_to.at[1], 0, 1)
        for slot, dy in ((0, 0), (1, -1), (2, 1)):
            add(pair.at[0], sides_to.at[slot], -1, dy)
            add(pair.at[1], sides_to.at[3 + slot], 1, dy)
        return out

    loads[4].wait()
    loads[5].wait()
    own[3] = land_v[...].astype(f32)
    packs[0], packs[1] = pack_sides([own[i] for i in range(4)])
    halo = halo_copies(own, packs, rows_in, sides_in, halo_send, halo_recv)
    for copy in halo:
        copy.start()
    recv_a[blk] = send_a[blk]
    recv_b[blk] = send_b[blk]

    loads[3].wait()
    tables(src_s, send_s, idcol, pick, back, listed)
    rscr[...] = jnp.zeros_like(rscr)
    loads[6].wait()
    loads[7].wait()
    turn_weights(w_v, wt_v)

    all_of(send_a, recv_a, a_recv).wait()
    push = remap(pick, recv_a, lhs, w_v)
    remap_back(own[3], temp_v[...], push[0] + push[1], wt_v, rscr, cscr, back, send2)
    send_all(send2, recv2, back_send, back_recv)
    recv2[blk] = send2[blk]

    all_of(send_b, recv_b, b_recv).wait()
    fown[0], fown[1] = remap(pick, recv_b, lhs, w_v)
    fpacks[0], fpacks[1] = pack_sides([fown[0], fown[1]])
    fhalo = halo_copies(fown, fpacks, frows_in, fsides_in, fhalo_send, fhalo_recv)
    for copy in fhalo:
        copy.start()

    for copy in halo:
        copy.wait_recv()
    around = [
        extend(own[i], rows_in[0, i], rows_in[1, i], [sides_in[j] for j in range(6)], i, 4) for i in range(4)
    ]
    for copy in fhalo:
        copy.wait_recv()
    push = [
        extend(fown[i], frows_in[0, i], frows_in[1, i], [fsides_in[j] for j in range(6)], i, 2) for i in range(2)
    ]
    subcycles(around, push, ocean_o)

    all_of(send2, recv2, back_recv).wait()
    gather_back(listed, recv2, atm_o)

    all_of(send_a, recv_a, a_send).wait()
    all_of(send_b, recv_b, b_send).wait()
    all_of(send2, recv2, back_send).wait()
    for copy in halo + fhalo:
        copy.wait_send()


def shards(ocean_state, sea_temp, land_mask, atm_flux, remap_w, source_tile, send_tiles, flux_mix):
    hbm = pl.BlockSpec(memory_space=pltpu.HBM)
    vmem = pl.BlockSpec(memory_space=pltpu.VMEM)
    message = pltpu.VMEM((N_BLK, MSG, TILE), bf16)
    dma = pltpu.SemaphoreType.DMA
    ocean, atm = pl.pallas_call(
        kernel,
        out_shape=(
            jax.ShapeDtypeStruct((3, OY, OX), f32),
            jax.ShapeDtypeStruct((2 * ATILES_DEV, TILE), f32),
        ),
        in_specs=[hbm] * 8,
        out_specs=(vmem, vmem),
        scratch_shapes=[
            pltpu.SMEM((KSRC, 2, OY), i32),
            pltpu.SMEM((1, CAP, 1, N_BLK), i32),
            pltpu.SMEM((3, FIELDS), f32),
            pltpu.VMEM((OY, 2, KSRC, TILE, TILE), bf16),
            pltpu.VMEM((OY, OX, KSRC * TILE), bf16),
            pltpu.VMEM((FIELDS, ATILES_DEV, TILE), bf16),
            pltpu.VMEM((OY, OX), f32),
            pltpu.VMEM((OY, OX), i32),
            pltpu.VMEM((4, OY, OX), f32),
            pltpu.VMEM((2, OY, OX), f32),
            pltpu.VMEM((N_BLK * MSG, TILE), i32),
            pltpu.VMEM((N_BLK * MSG, 2 * ATILES_DEV), bf16),
            message, message, message, message, message, message,
            pltpu.VMEM((2, OY, TILE), f32),
            pltpu.VMEM((2, OY, TILE), f32),
            pltpu.VMEM((2, 4, OY, OX), f32),
            pltpu.VMEM((2, 2, OY, OX), f32),
            pltpu.VMEM((6, OY, TILE), f32),
            pltpu.VMEM((6, OY, TILE), f32),
            pltpu.VMEM((REFS, TILE), i32),
            pltpu.VMEM((2 * REFS, N_BLK * MSG), bf16),
            pltpu.VMEM((N_BLK * MSG, 2 * TILE), bf16),
            pltpu.VMEM((2 * ATILES_DEV, N_BLK * MSG), bf16),
            pltpu.VMEM((4 * OY, KSRC * TILE), bf16),
            pltpu.VMEM((8 * OY, TILE), f32),
            pltpu.VMEM((4 * OY, KSRC * TILE), f32),
            dma((8,)),
            dma, dma, dma, dma, dma, dma,
            dma((8,)), dma((8,)), dma((8,)), dma((8,)),
        ],
        compiler_params=pltpu.CompilerParams(
            collective_id=0, has_side_effects=True, vmem_limit_bytes=32 * 1024 * 1024
        ),
    )(
        *(
            pltpu.with_memory_space_constraint(x, pltpu.HBM)
            for x in (
                ocean_state, sea_temp, land_mask,
                jnp.transpose(atm_flux[0], (1, 0, 2)),
                remap_w,
                jnp.transpose(source_tile, (2, 1, 0)),
                jnp.transpose(send_tiles, (0, 3, 1, 2)),
                flux_mix,
            )
        )
    )
    return ocean, atm.reshape(1, ATILES_DEV, 2, TILE)


def solution(mesh):
    placed = (
        P(None, ("comp", "sub"), "blk"),
        P(("comp", "sub"), "blk"),
        P(("comp", "sub"), "blk"),
        P(("comp", "sub"), "blk", None, None),
        P(("comp", "sub"), "blk", None, None, None),
        P(("comp", "sub"), "blk", None),
        P(("comp", "sub"), "blk", None, None),
        P(),
    )
    return jax.shard_map(
        shards,
        mesh=mesh,
        in_specs=placed,
        out_specs=(P(None, ("comp", "sub"), "blk"), P(("comp", "sub"), "blk", None, None)),
        check_vma=False,
    )
```

time: 51.8 us -> 43.9 us (0.85)
  Pallas kernels: 48 us -> 41.9 us
  local copies, waits for them, and re-layouts: 2.89 us -> 1.25 us
    pallas_call x1, Pallas kernels: 48 us -> 41.9 us  [shards(): pl.pallas_call(kernel, out_shape=(jax.ShapeDtypeStruct((3, OY, OX), f32),...]
    unnamed x2, local copies, waits for them, and re-layouts: 2.89 us -> 1.25 us
where the time goes in v2:
time: 43.9 us; the launch traced here: 43.8 us
  Pallas kernels  41.9 us (95%)
  local copies, waits for them, and re-layouts  1.25 us (3%)
  between operations  0.64 us (1%)
    pallas_call x1, Pallas kernels, shards(): pl.pallas_call(kernel, out_shape=(jax.ShapeDtypeStruct((3, OY, OX), f32),...  41.9 us
    unnamed x2, local copies, waits for them, and re-layouts  1.25 us

profile of v2, /device:TPU:1, one launch (start us, length us, event | category | flops | bytes accessed | tf_op | source)
XLA Modules:
  0.0 43.8 jit_solution(8943150564912436033)
XLA Ops:
  0.6 41.9 %shard_map.95 = (f32[3,16,256]{2,1,0:T(8,128)S(1)}, f32[128,128]{1,0:T(8,128)S(1)}) custom-call(f32[3,16,256]{2,1,0:T(8,128)} %state_h.1, f32[16,256]{1,0:T(8,128)} %temp_h.1, s32[16,256]{1,0:T(8,128)} %land_h.1, bf16[12,64,128]{2,1,0:T(8,128)(2,1)} %bitcast.7, bf16[16,2,3,128,128]{4,3,2,1,0:T(8,128)(2,1)} %w_h.1, s32[3,2,16]{2,1,0:T(2,128)} %bitcast.8, ...), custom_call_target="tpu_custom_call" | custom-call | tf_op jit(solution)/shard_map/pallas_call | solution.py:391
  42.6 0.6 %copy.12 = f32[3,16,256]{2,1,0:T(8,128)} copy(f32[3,16,256]{2,1,0:T(8,128)S(1)} %get-tuple-element.8) | data formatting | bytes 98304
  43.2 0.6 %copy.13 = f32[1,64,2,128]{3,2,1,0:T(2,128)} copy(f32[1,64,2,128]{3,2,1,0:T(2,128)S(1)} %bitcast.6) | data formatting | bytes 131072

commit v3 on v2

v3 whole, which is shorter than its diff:
```python
import functools

import jax
import jax.numpy as jnp
from jax import lax
from jax.experimental import pallas as pl
from jax.experimental.pallas import tpu as pltpu
from jax.sharding import PartitionSpec as P

MESH = pl.DeviceIdType.MESH

SUBCYCLES = 10
FIELDS = 12
TILE = 128
KSRC = 3
CAP = 3
OY = 16
OX = 256
ATILES_DEV = 64
N_BLK = 48
N_ROW = 16
N_SUB = 8

EXT_Y = 40
EXT_X = 384
PLANES = EXT_Y // 8
COLUMNS = EXT_X // TILE

PARTS = 4
MSG = CAP * PARTS
RET = CAP * 2
REFS = KSRC * OY * 2
ROWS = REFS * PARTS

drag_rate = 0.02
gravity_step = 0.6
depth_step = 0.6
force_step = 0.1
spread_rate = 0.1
filter_rate = 0.1

f32 = jnp.float32
bf16 = jnp.bfloat16
i32 = jnp.int32


def iota(shape, dim):
    return lax.broadcasted_iota(i32, shape, dim)


def pack_sides(fields):
    width = TILE // len(fields)
    lane = iota((OY, TILE), 1) // width
    first = last = jnp.zeros((OY, TILE), f32)
    for i, field in enumerate(fields):
        head, tail = field[:, :TILE], field[:, OX - TILE :]
        if i:
            head = pltpu.roll(head, i * width, 1)
        if i + 1 < len(fields):
            tail = pltpu.roll(tail, (i + 1) * width, 1)
        first = jnp.where(lane == i, head, first)
        last = jnp.where(lane == i, tail, last)
    return first, last


def extend(own, north, south, sides, i, count):
    width = TILE // count
    lane = iota((OY, TILE), 1)

    def beside(slot):
        east, west = sides[slot], sides[3 + slot]
        if i:
            east = pltpu.roll(east, TILE - i * width, 1)
        if i + 1 < count:
            west = pltpu.roll(west, TILE - (i + 1) * width, 1)
        return jnp.where(lane < TILE // 2, east, west)

    own = jnp.concatenate([own, beside(0)], axis=1)
    north = jnp.concatenate([north, beside(1)], axis=1)
    south = jnp.concatenate([south, beside(2)], axis=1)
    between = jnp.where(iota((8, EXT_X), 0) < 4, north[8:], south[:8])
    return jnp.concatenate([own, north[:8], between, south[8:]], axis=0)


def stage_tiles(flux_v, send_s, mix_s, listing, stage, send1):
    mixes = []
    for q in range(3):
        total = jnp.zeros((ATILES_DEV, TILE), f32)
        for f in range(FIELDS):
            total = total + mix_s[q, f] * flux_v[f].astype(f32)
        mixes.append(total)
    high = mixes[2].astype(bf16)
    rest = (mixes[2] - high.astype(f32)).astype(bf16)
    mixed = jnp.concatenate([mixes[0].astype(bf16), mixes[1].astype(bf16), high, rest], axis=0)

    upper = iota((8, TILE), 0) < PARTS
    for j in range(0, N_BLK, 2):
        slots = [send_s[0, s, 0, i] for i in (j, j + 1) for s in range(CAP)]
        for i in range(CAP):
            listing[pl.ds(j * MSG + i * 8, 8), :] = jnp.where(upper, slots[2 * i], slots[2 * i + 1])
    wanted = listing[...]
    part = iota((N_BLK * MSG, TILE), 0) % PARTS
    wanted = jnp.where(wanted >= 0, wanted + part * ATILES_DEV, -1)
    for c in range(2):
        stage[:, c * TILE : (c + 1) * TILE] = jnp.where(
            wanted == iota((N_BLK * MSG, TILE), 1) + c * TILE, 1.0, 0.0
        ).astype(bf16)
    rows = jnp.dot(stage[...], mixed, preferred_element_type=f32).astype(bf16)
    send1[...] = rows.reshape(send1.shape)


def tables(src_s, send_s, idcol, pick, back, listed):
    upper = iota((8, TILE), 0) < PARTS
    refs = jnp.full((1, TILE), -1, i32)
    wide = [jnp.full((1, TILE), -1, i32) for _ in range(2)]
    lane1 = iota((1, TILE), 1)
    for k in range(KSRC):
        for y in range(OY):
            both = [src_s[k, n, y] for n in range(2)]
            idcol[pl.ds((k * OY + y) * 8, 8), :] = jnp.where(upper, both[0], both[1])
            for n, value in enumerate(both):
                place = (k * OY + y) * 2 + n
                refs = jnp.where(lane1 == place, value, refs)
                wide[place // 64] = jnp.where(lane1 // 2 == place % 64, value, wide[place // 64])
    ids = idcol[...]
    spot = iota((ROWS, TILE), 0) // PARTS
    part = iota((ROWS, TILE), 0) % PARTS
    at = iota((ROWS, TILE), 1)
    again = jnp.max(jnp.where((ids == refs) & (spot < at), 1, 0), axis=0, keepdims=True)
    owners = ids // ATILES_DEV
    lower = (refs // ATILES_DEV == owners) & (refs < ids) & (again == 0) & (refs >= 0)
    rank = jnp.dot(
        jnp.where(lower, 1.0, 0.0).astype(bf16), jnp.ones((TILE, TILE), bf16), preferred_element_type=f32
    ).astype(i32)
    target = owners * MSG + rank * PARTS + part
    for c in range(0, N_BLK * MSG, TILE):
        width = min(TILE, N_BLK * MSG - c)
        pick[:, c : c + width] = jnp.where(target == at + c, 1.0, 0.0).astype(bf16)[:, :width]
    first = jnp.where(part == 0, rank, 0)
    for c in range(2):
        rank_line = jnp.sum(jnp.where(spot == at // 2 + c * 64, first, 0), axis=0, keepdims=True)
        to = (wide[c] // ATILES_DEV) * RET + rank_line * 2 + lane1 % 2
        to = jnp.where(wide[c] >= 0, to, -1)
        back[:, c * TILE : (c + 1) * TILE] = jnp.where(to == iota((N_BLK * RET, TILE), 0), 1.0, 0.0).astype(bf16)
    slot = [jnp.full((1, TILE), -1, i32) for _ in range(3)]
    for j in range(N_BLK):
        for s in range(CAP):
            place = j * CAP + s
            slot[place // 64] = jnp.where(lane1 // 2 == place % 64, send_s[0, s, 0, j], slot[place // 64])
    for c in range(3):
        width = min(TILE, N_BLK * RET - c * TILE)
        hit = slot[c] * 2 + lane1 % 2 == iota((2 * ATILES_DEV, TILE), 0)
        listed[:, c * TILE : c * TILE + width] = jnp.where(hit, 1.0, 0.0).astype(bf16)[:, :width]


def weights(w_v, y):
    return jnp.concatenate([w_v[y, n].reshape(KSRC * TILE, TILE) for n in range(2)], axis=1)


def turn_weights(w_v, wt_v):
    for y in range(OY):
        wt_v[y] = weights(w_v, y).T


def remap(pick, recv1, lhs, w_v, fscr):
    arrived = recv1[...].reshape(N_BLK * MSG, TILE)
    picked = jnp.dot(pick[...], arrived, preferred_element_type=f32).astype(bf16)
    lhs[...] = jnp.concatenate([picked[k * TILE : (k + 1) * TILE] for k in range(KSRC)], axis=1)
    for y in range(OY):
        out = jnp.dot(lhs[pl.ds(y // 2 * 16, 16), :], weights(w_v, y), preferred_element_type=f32)
        for n in range(2):
            fscr[pl.ds(n * TILE + y * 8, 8), :] = out[y % 2 * 8 : y % 2 * 8 + 8, n * TILE : (n + 1) * TILE]
    return [
        jnp.concatenate(
            [fscr[pl.ds(n * (TILE + PARTS) + p, OY, stride=8), :] for n in range(2)], axis=1
        )
        for p in range(PARTS)
    ]


def remap_back(sea, temp, push, wt_v, rscr, cscr, back, send2):
    surface = sea * (temp + push)
    ice = sea * jax.nn.sigmoid(-2.0 * (surface + 1.0))
    for f, field in enumerate((surface, ice)):
        field = field.astype(bf16).astype(f32)
        for n in range(2):
            rscr[pl.ds(n * 4 * OY + 2 * n + f, OY, stride=4), :] = field[:, n * TILE : (n + 1) * TILE]
    returned = jnp.concatenate([rscr[: 4 * OY], rscr[4 * OY :]], axis=1).astype(bf16)
    for y in range(OY):
        out = jnp.dot(returned[y // 4 * 16 : y // 4 * 16 + 16], wt_v[y], preferred_element_type=f32)
        cscr[pl.ds(y * 4, 4), :] = out[y % 4 * 4 : y % 4 * 4 + 4]
    terms = jnp.concatenate([cscr[:, k * TILE : (k + 1) * TILE] for k in range(KSRC)], axis=0)
    table = back[:, : 4 * OY * KSRC]
    top = terms.astype(bf16)
    rest = (terms - top.astype(f32)).astype(bf16)
    sums = jnp.dot(table, top, preferred_element_type=f32) + jnp.dot(table, rest, preferred_element_type=f32)
    send2[...] = sums.astype(bf16).reshape(send2.shape)


def gather_back(listed, recv2, atm_o):
    atm_o[...] = jnp.dot(listed[...], recv2[...].reshape(N_BLK * RET, TILE), preferred_element_type=f32)


def reorder(fields, table):
    rows = jnp.concatenate(fields, axis=0)
    top = rows.astype(bf16)
    rest = (rows - top.astype(f32)).astype(bf16)
    table = table[...]
    out = jnp.dot(top, table, preferred_element_type=f32) + jnp.dot(rest, table, preferred_element_type=f32)
    size = fields[0].shape[0]
    return [out[i * size : (i + 1) * size] for i in range(len(fields))]


def column_tables(spread, gather):
    lane = iota((EXT_X, TILE), 1)
    for t in range(COLUMNS):
        spread[:, t * TILE : (t + 1) * TILE] = jnp.where(
            iota((EXT_X, TILE), 0) == lane * COLUMNS + t, 1.0, 0.0
        ).astype(bf16)
    spot = iota((EXT_X, OX), 0)
    spot = spot % TILE * COLUMNS + spot // TILE
    gather[...] = jnp.where(spot == iota((EXT_X, OX), 1), 1.0, 0.0).astype(bf16)


def interleave(fields, rows, spread):
    out = []
    for i, field in enumerate(reorder(fields, spread)):
        for t in range(COLUMNS):
            rows[i, pl.ds(t * EXT_Y, EXT_Y), :] = field[:, t * TILE : (t + 1) * TILE]
        out.append(
            [
                jnp.concatenate(
                    [rows[i, pl.ds(t * EXT_Y + v, 8, stride=PLANES), :] for t in range(COLUMNS)], axis=1
                )
                for v in range(PLANES)
            ]
        )
    return out


def own_cells(fields, rows, gather):
    out = []
    for i, planes in enumerate(fields):
        for t in range(COLUMNS):
            for v in range(PLANES):
                rows[i, pl.ds(t * EXT_Y + v, 8, stride=PLANES), :] = planes[v][:, t * TILE : (t + 1) * TILE]
        out.append(jnp.concatenate([rows[i, pl.ds(t * EXT_Y, OY), :] for t in range(COLUMNS)], axis=1))
    return reorder(out, gather)


def from_east(planes):
    return [jnp.concatenate([x[:, TILE:], pltpu.roll(x[:, :TILE], TILE - 1, 1)], axis=1) for x in planes]


def from_west(planes):
    return [
        jnp.concatenate([pltpu.roll(x[:, EXT_X - TILE :], 1, 1), x[:, : EXT_X - TILE]], axis=1) for x in planes
    ]


def from_north(planes):
    return planes[1:] + [pltpu.roll(planes[0], 7, 0)]


def from_south(planes):
    return [pltpu.roll(planes[-1], 1, 0)] + planes[:-1]


def each(f, *fields):
    return [f(*planes) for planes in zip(*fields)]


CARRY = depth_step * (1.0 - drag_rate)


def start_ocean(around, rows, spread, masks, state):
    eta, east, north, sea = interleave(around, rows, spread)
    east_open = each(lambda a, b: a * b, sea, from_east(sea))
    north_open = each(lambda a, b: a * b, sea, from_north(sea))
    consts = [
        sea,
        each(lambda m: (gravity_step * depth_step) * m, east_open),
        each(lambda m: (gravity_step * depth_step) * m, north_open),
        each(lambda m: (filter_rate * (1.0 - drag_rate)) * m, east_open),
        each(lambda m: (filter_rate * (1.0 - drag_rate)) * m, north_open),
    ]
    consts += [from_west(consts[1]), from_west(consts[3])]
    east = each(lambda m, w: CARRY * m * w, east_open, east)
    north = each(lambda m, w: CARRY * m * w, north_open, north)
    for ref, fields in ((masks, consts), (state, [eta, east, from_west(east), north])):
        for i, planes in enumerate(fields):
            for v in range(PLANES):
                ref[i, v] = planes[v]


def subcycles(push, rows, spread, gather, masks, state, ocean_o):
    push = interleave(push, rows, spread)
    sea, grad_e, grad_n, keep_e, keep_n, grad_w, keep_w = (
        [masks[i, v] for v in range(PLANES)] for i in range(7)
    )
    push_e, push_n = (
        each(lambda m, f: (force_step / gravity_step) * m * f, grad, field)
        for grad, field in zip((grad_e, grad_n), push)
    )
    push_w = from_west(push_e)
    share = spread_rate / (gravity_step * depth_step)
    centre = (1.0 - 4.0 * filter_rate) / filter_rate

    def advance(_, carried):
        eta, east, west, north = (list(field) for field in carried)
        slope_e = each(lambda m, a, b: m * (a - b), grad_e, from_east(eta), eta)
        slope_w = each(lambda m, a, b: m * (a - b), grad_w, eta, from_west(eta))
        slope_n = each(lambda m, a, b: m * (a - b), grad_n, from_north(eta), eta)
        east = each(lambda w, p, a: w + p - a, east, push_e, slope_e)
        west = each(lambda w, p, a: w + p - a, west, push_w, slope_w)
        north = each(lambda w, p, a: w + p - a, north, push_n, slope_n)
        flow_n = each(lambda w, a: w - share * a, north, slope_n)
        eta = each(
            lambda m, e, a, b, x, y, c, d: m * (e - ((a - b) - share * (x - y)) - (c - d)),
            sea, eta, east, west, slope_e, slope_w, flow_n, from_south(flow_n),
        )

        def smooth(m, x, beside_e, beside_w):
            return each(
                lambda m, x, a, b, c, d: m * (centre * x + ((a + b) + (c + d))),
                m, x, beside_e, beside_w, from_north(x), from_south(x),
            )

        return (
            tuple(eta),
            tuple(smooth(keep_e, east, from_east(east), west)),
            tuple(smooth(keep_w, west, east, from_west(west))),
            tuple(smooth(keep_n, north, from_east(north), from_west(north))),
        )

    first = tuple(tuple(state[i, v] for v in range(PLANES)) for i in range(4))
    last = lax.fori_loop(0, SUBCYCLES, advance, first, unroll=True)
    last = (last[0], last[1], last[3])
    cells = own_cells(last, rows, gather)
    for i, scale in enumerate((1.0, 1.0 / CARRY, 1.0 / CARRY)):
        ocean_o[i] = scale * cells[i]


def kernel(
    state_h, temp_h, land_h, flux_h, w_h, src_h, send_h, mix_h,
    ocean_o, atm_o,
    src_s, send_s, mix_s,
    w_v, wt_v, flux_v, temp_v, land_v, own, fown,
    listing, stage, send1, recv1, send2, recv2,
    packs, fpacks, rows_in, frows_in, sides_in, fsides_in,
    idcol, pick, back, listed, lhs, fscr, rscr, cscr, rows, masks, state, spread, gather,
    load_sem, tile_send, tile_recv, back_send, back_recv,
    halo_send, halo_recv, fhalo_send, fhalo_recv,
):
    comp = lax.axis_index("comp")
    blk = lax.axis_index("blk")
    sub = lax.axis_index("sub")
    row = comp * N_SUB + sub

    def device(dx, dy):
        to_row = lax.rem(row + dy + N_ROW, N_ROW)
        return (to_row // N_SUB, lax.rem(blk + dx + N_BLK, N_BLK), lax.rem(to_row, N_SUB))

    def partner(i):
        away = N_BLK // 2 + (1 - 2 * lax.rem(i + comp, 2)) * (i // 2)
        return lax.rem(blk + away, N_BLK)

    barrier = pltpu.get_barrier_semaphore()

    def greet(i, carry):
        pl.semaphore_signal(barrier, inc=1, device_id=(comp, partner(i), sub), device_id_type=MESH)
        return carry

    lax.fori_loop(1, N_BLK, greet, 0)
    for dx, dy in ((0, 1), (0, -1), (1, 1), (1, -1), (-1, 1), (-1, -1)):
        pl.semaphore_signal(barrier, inc=1, device_id=device(dx, dy), device_id_type=MESH)

    loads = [
        pltpu.make_async_copy(src, dst, load_sem.at[i])
        for i, (src, dst) in enumerate(
            [
                (mix_h, mix_s), (flux_h, flux_v), (send_h, send_s), (src_h, src_s),
                (state_h, own.at[pl.ds(0, 3)]), (land_h, land_v), (temp_h, temp_v), (w_h, w_v),
            ]
        )
    ]
    for load in loads:
        load.start()

    for load in loads[:3]:
        load.wait()
    stage_tiles(flux_v, send_s, mix_s, listing, stage, send1)

    pl.semaphore_wait(barrier, N_BLK - 1 + 6)

    def send_all(src, dst, send_sem, recv_sem):
        def send(i, carry):
            pltpu.make_async_remote_copy(
                src_ref=src.at[partner(i)], dst_ref=dst.at[blk],
                send_sem=send_sem, recv_sem=recv_sem,
                device_id=(comp, partner(i), sub), device_id_type=MESH,
            ).start()
            return carry

        lax.fori_loop(1, N_BLK, send, 0)

    others = pl.ds(0, N_BLK - 1)

    def all_of(src, dst, sem):
        return pltpu.make_async_copy(src.at[others], dst.at[others], sem)

    send_all(send1, recv1, tile_send, tile_recv)

    def halo_copies(block, pair, rows_to, sides_to, send_sem, recv_sem):
        out = []

        def add(src, dst, dx, dy):
            i = len(out)
            out.append(
                pltpu.make_async_remote_copy(
                    src_ref=src, dst_ref=dst, send_sem=send_sem.at[i], recv_sem=recv_sem.at[i],
                    device_id=device(dx, dy), device_id_type=MESH,
                )
            )

        add(block, rows_to.at[0], 0, -1)
        add(block, rows_to.at[1], 0, 1)
        for slot, dy in ((0, 0), (1, -1), (2, 1)):
            add(pair.at[0], sides_to.at[slot], -1, dy)
            add(pair.at[1], sides_to.at[3 + slot], 1, dy)
        return out

    loads[4].wait()
    loads[5].wait()
    own[3] = land_v[...].astype(f32)
    packs[0], packs[1] = pack_sides([own[i] for i in range(4)])
    halo = halo_copies(own, packs, rows_in, sides_in, halo_send, halo_recv)
    for copy in halo:
        copy.start()
    recv1[blk] = send1[blk]

    loads[3].wait()
    tables(src_s, send_s, idcol, pick, back, listed)
    column_tables(spread, gather)
    rscr[...] = jnp.zeros_like(rscr)
    loads[6].wait()
    loads[7].wait()
    turn_weights(w_v, wt_v)

    all_of(send1, recv1, tile_recv).wait()
    forcing = remap(pick, recv1, lhs, w_v, fscr)
    fown[0], fown[1] = forcing[0], forcing[1]
    fpacks[0], fpacks[1] = pack_sides(forcing[:2])
    fhalo = halo_copies(fown, fpacks, frows_in, fsides_in, fhalo_send, fhalo_recv)
    for copy in fhalo:
        copy.start()
    remap_back(own[3], temp_v[...], forcing[2] + forcing[3], wt_v, rscr, cscr, back, send2)
    send_all(send2, recv2, back_send, back_recv)
    recv2[blk] = send2[blk]

    for copy in halo:
        copy.wait_recv()
    around = [
        extend(own[i], rows_in[0, i], rows_in[1, i], [sides_in[j] for j in range(6)], i, 4) for i in range(4)
    ]
    start_ocean(around, rows, spread, masks, state)
    for copy in fhalo:
        copy.wait_recv()
    push = [
        extend(fown[i], frows_in[0, i], frows_in[1, i], [fsides_in[j] for j in range(6)], i, 2) for i in range(2)
    ]
    subcycles(push, rows, spread, gather, masks, state, ocean_o)

    all_of(send2, recv2, back_recv).wait()
    gather_back(listed, recv2, atm_o)

    all_of(send1, recv1, tile_send).wait()
    all_of(send2, recv2, back_send).wait()
    for copy in halo + fhalo:
        copy.wait_send()


def shards(ocean_state, sea_temp, land_mask, atm_flux, remap_w, source_tile, send_tiles, flux_mix):
    hbm = pl.BlockSpec(memory_space=pltpu.HBM)
    vmem = pl.BlockSpec(memory_space=pltpu.VMEM)
    message = pltpu.VMEM((N_BLK, CAP, PARTS, TILE), bf16)
    returned = pltpu.VMEM((N_BLK, CAP, 2, TILE), bf16)
    dma = pltpu.SemaphoreType.DMA
    ocean, atm = pl.pallas_call(
        kernel,
        out_shape=(
            jax.ShapeDtypeStruct((3, OY, OX), f32),
            jax.ShapeDtypeStruct((2 * ATILES_DEV, TILE), f32),
        ),
        in_specs=[hbm] * 8,
        out_specs=(vmem, vmem),
        scratch_shapes=[
            pltpu.SMEM((KSRC, 2, OY), i32),
            pltpu.SMEM((1, CAP, 1, N_BLK), i32),
            pltpu.SMEM((3, FIELDS), f32),
            pltpu.VMEM((OY, 2, KSRC, TILE, TILE), bf16),
            pltpu.VMEM((OY, OX, KSRC * TILE), bf16),
            pltpu.VMEM((FIELDS, ATILES_DEV, TILE), bf16),
            pltpu.VMEM((OY, OX), f32),
            pltpu.VMEM((OY, OX), i32),
            pltpu.VMEM((4, OY, OX), f32),
            pltpu.VMEM((2, OY, OX), f32),
            pltpu.VMEM((N_BLK * MSG, TILE), i32),
            pltpu.VMEM((N_BLK * MSG, 4 * ATILES_DEV), bf16),
            message, message, returned, returned,
            pltpu.VMEM((2, OY, TILE), f32),
            pltpu.VMEM((2, OY, TILE), f32),
            pltpu.VMEM((2, 4, OY, OX), f32),
            pltpu.VMEM((2, 2, OY, OX), f32),
            pltpu.VMEM((6, OY, TILE), f32),
            pltpu.VMEM((6, OY, TILE), f32),
            pltpu.VMEM((ROWS, TILE), i32),
            pltpu.VMEM((ROWS, N_BLK * MSG), bf16),
            pltpu.VMEM((N_BLK * RET, 2 * TILE), bf16),
            pltpu.VMEM((2 * ATILES_DEV, N_BLK * RET), bf16),
            pltpu.VMEM((TILE, KSRC * TILE), bf16),
            pltpu.VMEM((2 * TILE, TILE), f32),
            pltpu.VMEM((8 * OY, TILE), f32),
            pltpu.VMEM((4 * OY, KSRC * TILE), f32),
            pltpu.VMEM((4, COLUMNS * EXT_Y, TILE), f32),
            pltpu.VMEM((7, PLANES, 8, EXT_X), f32),
            pltpu.VMEM((4, PLANES, 8, EXT_X), f32),
            pltpu.VMEM((EXT_X, EXT_X), bf16),
            pltpu.VMEM((EXT_X, OX), bf16),
            dma((8,)),
            dma, dma, dma, dma,
            dma((8,)), dma((8,)), dma((8,)), dma((8,)),
        ],
        compiler_params=pltpu.CompilerParams(
            collective_id=0, has_side_effects=True, vmem_limit_bytes=32 * 1024 * 1024
        ),
    )(
        *(
            pltpu.with_memory_space_constraint(x, pltpu.HBM)
            for x in (
                ocean_state, sea_temp, land_mask,
                jnp.transpose(atm_flux[0], (1, 0, 2)),
                remap_w,
                jnp.transpose(source_tile, (2, 1, 0)),
                jnp.transpose(send_tiles, (0, 3, 1, 2)),
                flux_mix,
            )
        )
    )
    return ocean, atm.reshape(1, ATILES_DEV, 2, TILE)


def solution(mesh):
    placed = (
        P(None, ("comp", "sub"), "blk"),
        P(("comp", "sub"), "blk"),
        P(("comp", "sub"), "blk"),
        P(("comp", "sub"), "blk", None, None),
        P(("comp", "sub"), "blk", None, None, None),
        P(("comp", "sub"), "blk", None),
        P(("comp", "sub"), "blk", None, None),
        P(),
    )
    return jax.shard_map(
        shards,
        mesh=mesh,
        in_specs=placed,
        out_specs=(P(None, ("comp", "sub"), "blk"), P(("comp", "sub"), "blk", None, None)),
        check_vma=False,
    )
```

time: 43.9 us -> 40.4 us (0.920)
  Pallas kernels: 41.9 us -> 38.4 us
    pallas_call x1, Pallas kernels: 41.9 us -> 38.4 us  [shards(): pl.pallas_call(kernel, out_shape=(jax.ShapeDtypeStruct((3, OY, OX), f32),...]
where the time goes in v3:
time: 40.4 us; the launch traced here: 40.3 us
  Pallas kernels  38.4 us (95%)
  local copies, waits for them, and re-layouts  1.25 us (3%)
  between operations  0.64 us (2%)
    pallas_call x1, Pallas kernels, shards(): pl.pallas_call(kernel, out_shape=(jax.ShapeDtypeStruct((3, OY, OX), f32),...  38.4 us
    unnamed x2, local copies, waits for them, and re-layouts  1.25 us

profile of v3, /device:TPU:1, one launch (start us, length us, event | category | flops | bytes accessed | tf_op | source)
XLA Modules:
  0.0 40.3 jit_solution(13266570496649332948)
XLA Ops:
  0.6 38.4 %shard_map.95 = (f32[3,16,256]{2,1,0:T(8,128)S(1)}, f32[128,128]{1,0:T(8,128)S(1)}) custom-call(f32[3,16,256]{2,1,0:T(8,128)} %state_h.1, f32[16,256]{1,0:T(8,128)} %temp_h.1, s32[16,256]{1,0:T(8,128)} %land_h.1, bf16[12,64,128]{2,1,0:T(8,128)(2,1)} %bitcast.7, bf16[16,2,3,128,128]{4,3,2,1,0:T(8,128)(2,1)} %w_h.1, s32[3,2,16]{2,1,0:T(2,128)} %bitcast.8, ...), custom_call_target="tpu_custom_call" | custom-call | tf_op jit(solution)/shard_map/pallas_call | solution.py:489
  39.0 0.6 %copy.12 = f32[3,16,256]{2,1,0:T(8,128)} copy(f32[3,16,256]{2,1,0:T(8,128)S(1)} %get-tuple-element.8) | data formatting | bytes 98304
  39.6 0.6 %copy.13 = f32[1,64,2,128]{3,2,1,0:T(2,128)} copy(f32[1,64,2,128]{3,2,1,0:T(2,128)S(1)} %bitcast.6) | data formatting | bytes 131072

commit v4 on v3

--- a/solution.py
+++ b/solution.py
@@ -158,18 +158,25 @@
 
 
 def turn_weights(w_v, wt_v):
-    for y in range(OY):
-        wt_v[y] = weights(w_v, y).T
+    for y in range(0, OY, 2):
+        for i in range(2):
+            wt_v[y // 2, :, i * KSRC * TILE : (i + 1) * KSRC * TILE] = weights(w_v, y + i).T
 
 
 def remap(pick, recv1, lhs, w_v, fscr):
     arrived = recv1[...].reshape(N_BLK * MSG, TILE)
     picked = jnp.dot(pick[...], arrived, preferred_element_type=f32).astype(bf16)
     lhs[...] = jnp.concatenate([picked[k * TILE : (k + 1) * TILE] for k in range(KSRC)], axis=1)
-    for y in range(OY):
-        out = jnp.dot(lhs[pl.ds(y // 2 * 16, 16), :], weights(w_v, y), preferred_element_type=f32)
+    upper = iota((16, KSRC * TILE), 0) < 8
+    for y in range(0, OY, 2):
+        both = lhs[pl.ds(y * 8, 16), :]
+        halves = [jnp.where(upper, both, 0), jnp.where(upper, 0, both)]
+        out = jnp.dot(
+            jnp.concatenate(halves, axis=1), jnp.concatenate([weights(w_v, y), weights(w_v, y + 1)], axis=0),
+            preferred_element_type=f32,
+        )
         for n in range(2):
-            fscr[pl.ds(n * TILE + y * 8, 8), :] = out[y % 2 * 8 : y % 2 * 8 + 8, n * TILE : (n + 1) * TILE]
+            fscr[pl.ds(n * TILE + y * 8, 16), :] = out[:, n * TILE : (n + 1) * TILE]
     return [
         jnp.concatenate(
             [fscr[pl.ds(n * (TILE + PARTS) + p, OY, stride=8), :] for n in range(2)], axis=1
@@ -186,9 +193,11 @@
         for n in range(2):
             rscr[pl.ds(n * 4 * OY + 2 * n + f, OY, stride=4), :] = field[:, n * TILE : (n + 1) * TILE]
     returned = jnp.concatenate([rscr[: 4 * OY], rscr[4 * OY :]], axis=1).astype(bf16)
-    for y in range(OY):
-        out = jnp.dot(returned[y // 4 * 16 : y // 4 * 16 + 16], wt_v[y], preferred_element_type=f32)
-        cscr[pl.ds(y * 4, 4), :] = out[y % 4 * 4 : y % 4 * 4 + 4]
+    for y in range(0, OY, 2):
+        out = jnp.dot(returned[y // 4 * 16 : y // 4 * 16 + 16], wt_v[y // 2], preferred_element_type=f32)
+        for i in range(2):
+            start = (y + i) % 4 * 4
+            cscr[pl.ds((y + i) * 4, 4), :] = out[start : start + 4, i * KSRC * TILE : (i + 1) * KSRC * TILE]
     terms = jnp.concatenate([cscr[:, k * TILE : (k + 1) * TILE] for k in range(KSRC)], axis=0)
     table = back[:, : 4 * OY * KSRC]
     top = terms.astype(bf16)
@@ -350,7 +359,7 @@
     packs, fpacks, rows_in, frows_in, sides_in, fsides_in,
     idcol, pick, back, listed, lhs, fscr, rscr, cscr, rows, masks, state, spread, gather,
     load_sem, tile_send, tile_recv, back_send, back_recv,
-    halo_send, halo_recv, fhalo_send, fhalo_recv,
+    halo_send, halo_recv, fhalo_send, fhalo_recv, ready,
 ):
     comp = lax.axis_index("comp")
     blk = lax.axis_index("blk")
@@ -372,8 +381,8 @@
         return carry
 
     lax.fori_loop(1, N_BLK, greet, 0)
-    for dx, dy in ((0, 1), (0, -1), (1, 1), (1, -1), (-1, 1), (-1, -1)):
-        pl.semaphore_signal(barrier, inc=1, device_id=device(dx, dy), device_id_type=MESH)
+    for dy in (1, -1):
+        pl.semaphore_signal(barrier, inc=1, device_id=device(0, dy), device_id_type=MESH)
 
     loads = [
         pltpu.make_async_copy(src, dst, load_sem.at[i])
@@ -391,7 +400,9 @@
         load.wait()
     stage_tiles(flux_v, send_s, mix_s, listing, stage, send1)
 
-    pl.semaphore_wait(barrier, N_BLK - 1 + 6)
+    pl.semaphore_wait(barrier, N_BLK - 1 + 2)
+    for dy in (1, -1):
+        pl.semaphore_signal(ready, inc=1, device_id=device(0, dy), device_id_type=MESH)
 
     def send_all(src, dst, send_sem, recv_sem):
         def send(i, carry):
@@ -434,9 +445,6 @@
     loads[5].wait()
     own[3] = land_v[...].astype(f32)
     packs[0], packs[1] = pack_sides([own[i] for i in range(4)])
-    halo = halo_copies(own, packs, rows_in, sides_in, halo_send, halo_recv)
-    for copy in halo:
-        copy.start()
     recv1[blk] = send1[blk]
 
     loads[3].wait()
@@ -446,6 +454,10 @@
     loads[6].wait()
     loads[7].wait()
     turn_weights(w_v, wt_v)
+    pl.semaphore_wait(ready, 2)
+    halo = halo_copies(own, packs, rows_in, sides_in, halo_send, halo_recv)
+    for copy in halo:
+        copy.start()
 
     all_of(send1, recv1, tile_recv).wait()
     forcing = remap(pick, recv1, lhs, w_v, fscr)
@@ -499,7 +511,7 @@
             pltpu.SMEM((1, CAP, 1, N_BLK), i32),
             pltpu.SMEM((3, FIELDS), f32),
             pltpu.VMEM((OY, 2, KSRC, TILE, TILE), bf16),
-            pltpu.VMEM((OY, OX, KSRC * TILE), bf16),
+            pltpu.VMEM((OY // 2, OX, 2 * KSRC * TILE), bf16),
             pltpu.VMEM((FIELDS, ATILES_DEV, TILE), bf16),
             pltpu.VMEM((OY, OX), f32),
             pltpu.VMEM((OY, OX), i32),
@@ -530,6 +542,7 @@
             dma((8,)),
             dma, dma, dma, dma,
             dma((8,)), dma((8,)), dma((8,)), dma((8,)),
+            pltpu.SemaphoreType.REGULAR,
         ],
         compiler_params=pltpu.CompilerParams(
             collective_id=0, has_side_effects=True, vmem_limit_bytes=32 * 1024 * 1024

time: 40.4 us -> 39.8 us (0.985)
  Pallas kernels: 38.4 us -> 37.8 us
    pallas_call x1, Pallas kernels: 38.4 us -> 37.8 us  [shards(): pl.pallas_call(kernel, out_shape=(jax.ShapeDtypeStruct((3, OY, OX), f32),...]
where the time goes in v4:
time: 39.8 us; the launch traced here: 39.7 us
  Pallas kernels  37.8 us (95%)
  local copies, waits for them, and re-layouts  1.25 us (3%)
  between operations  0.64 us (2%)
    pallas_call x1, Pallas kernels, shards(): pl.pallas_call(kernel, out_shape=(jax.ShapeDtypeStruct((3, OY, OX), f32),...  37.8 us
    unnamed x2, local copies, waits for them, and re-layouts  1.25 us

profile of v4, /device:TPU:1, one launch (start us, length us, event | category | flops | bytes accessed | tf_op | source)
XLA Modules:
  0.0 39.7 jit_solution(16700065573672591842)
XLA Ops:
  0.6 37.8 %shard_map.95 = (f32[3,16,256]{2,1,0:T(8,128)S(1)}, f32[128,128]{1,0:T(8,128)S(1)}) custom-call(f32[3,16,256]{2,1,0:T(8,128)} %state_h.1, f32[16,256]{1,0:T(8,128)} %temp_h.1, s32[16,256]{1,0:T(8,128)} %land_h.1, bf16[12,64,128]{2,1,0:T(8,128)(2,1)} %bitcast.7, bf16[16,2,3,128,128]{4,3,2,1,0:T(8,128)(2,1)} %w_h.1, s32[3,2,16]{2,1,0:T(2,128)} %bitcast.8, ...), custom_call_target="tpu_custom_call" | custom-call | tf_op jit(solution)/shard_map/pallas_call | solution.py:501
  38.5 0.6 %copy.12 = f32[3,16,256]{2,1,0:T(8,128)} copy(f32[3,16,256]{2,1,0:T(8,128)S(1)} %get-tuple-element.8) | data formatting | bytes 98304
  39.1 0.6 %copy.13 = f32[1,64,2,128]{3,2,1,0:T(2,128)} copy(f32[1,64,2,128]{3,2,1,0:T(2,128)S(1)} %bitcast.6) | data formatting | bytes 131072

commit v5 on v4

--- a/solution.py
+++ b/solution.py
@@ -192,7 +192,7 @@
         field = field.astype(bf16).astype(f32)
         for n in range(2):
             rscr[pl.ds(n * 4 * OY + 2 * n + f, OY, stride=4), :] = field[:, n * TILE : (n + 1) * TILE]
-    returned = jnp.concatenate([rscr[: 4 * OY], rscr[4 * OY :]], axis=1).astype(bf16)
+    returned = jnp.concatenate([rscr[: 4 * OY], rscr[4 * OY : 8 * OY]], axis=1).astype(bf16)
     for y in range(0, OY, 2):
         out = jnp.dot(returned[y // 4 * 16 : y // 4 * 16 + 16], wt_v[y // 2], preferred_element_type=f32)
         for i in range(2):
@@ -214,8 +214,9 @@
     rows = jnp.concatenate(fields, axis=0)
     top = rows.astype(bf16)
     rest = (rows - top.astype(f32)).astype(bf16)
-    table = table[...]
-    out = jnp.dot(top, table, preferred_element_type=f32) + jnp.dot(rest, table, preferred_element_type=f32)
+    out = jnp.dot(
+        jnp.concatenate([top, rest], axis=1), jnp.concatenate([table[...]] * 2, axis=0), preferred_element_type=f32
+    )
     size = fields[0].shape[0]
     return [out[i * size : (i + 1) * size] for i in range(len(fields))]
 
@@ -302,7 +303,7 @@
                 ref[i, v] = planes[v]
 
 
-def subcycles(push, rows, spread, gather, masks, state, ocean_o):
+def subcycles(push, rows, spread, masks, state):
     push = interleave(push, rows, spread)
     sea, grad_e, grad_n, keep_e, keep_n, grad_w, keep_w = (
         [masks[i, v] for v in range(PLANES)] for i in range(7)
@@ -344,7 +345,10 @@
 
     first = tuple(tuple(state[i, v] for v in range(PLANES)) for i in range(4))
     last = lax.fori_loop(0, SUBCYCLES, advance, first, unroll=True)
-    last = (last[0], last[1], last[3])
+    return last[0], last[1], last[3]
+
+
+def store_ocean(last, rows, gather, ocean_o):
     cells = own_cells(last, rows, gather)
     for i, scale in enumerate((1.0, 1.0 / CARRY, 1.0 / CARRY)):
         ocean_o[i] = scale * cells[i]
@@ -434,11 +438,11 @@
                 )
             )
 
+        for slot, dy in ((1, -1), (2, 1), (0, 0)):
+            add(pair.at[0], sides_to.at[slot], -1, dy)
+            add(pair.at[1], sides_to.at[3 + slot], 1, dy)
         add(block, rows_to.at[0], 0, -1)
         add(block, rows_to.at[1], 0, 1)
-        for slot, dy in ((0, 0), (1, -1), (2, 1)):
-            add(pair.at[0], sides_to.at[slot], -1, dy)
-            add(pair.at[1], sides_to.at[3 + slot], 1, dy)
         return out
 
     loads[4].wait()
@@ -481,9 +485,10 @@
     push = [
         extend(fown[i], frows_in[0, i], frows_in[1, i], [fsides_in[j] for j in range(6)], i, 2) for i in range(2)
     ]
-    subcycles(push, rows, spread, gather, masks, state, ocean_o)
+    last = subcycles(push, rows, spread, masks, state)
 
     all_of(send2, recv2, back_recv).wait()
+    store_ocean(last, rows, gather, ocean_o)
     gather_back(listed, recv2, atm_o)
 
     all_of(send1, recv1, tile_send).wait()
@@ -531,10 +536,10 @@
             pltpu.VMEM((N_BLK * RET, 2 * TILE), bf16),
             pltpu.VMEM((2 * ATILES_DEV, N_BLK * RET), bf16),
             pltpu.VMEM((TILE, KSRC * TILE), bf16),
-            pltpu.VMEM((2 * TILE, TILE), f32),
-            pltpu.VMEM((8 * OY, TILE), f32),
+            pltpu.VMEM((2 * TILE + 8, TILE), f32),
+            pltpu.VMEM((8 * OY + 8, TILE), f32),
             pltpu.VMEM((4 * OY, KSRC * TILE), f32),
-            pltpu.VMEM((4, COLUMNS * EXT_Y, TILE), f32),
+            pltpu.VMEM((4, COLUMNS * EXT_Y + 8, TILE), f32),
             pltpu.VMEM((7, PLANES, 8, EXT_X), f32),
             pltpu.VMEM((4, PLANES, 8, EXT_X), f32),
             pltpu.VMEM((EXT_X, EXT_X), bf16),

time: 39.8 us -> 39.6 us (level)
  no operation moved by 1% of the time
where the time goes in v5:
time: 39.6 us; the launch traced here: 39.5 us
  Pallas kernels  37.6 us (95%)
  local copies, waits for them, and re-layouts  1.25 us (3%)
  between operations  0.64 us (2%)
    pallas_call x1, Pallas kernels, shards(): pl.pallas_call(kernel, out_shape=(jax.ShapeDtypeStruct((3, OY, OX), f32),...  37.6 us
    unnamed x2, local copies, waits for them, and re-layouts  1.25 us

profile of v5, /device:TPU:1, one launch (start us, length us, event | category | flops | bytes accessed | tf_op | source)
XLA Modules:
  0.0 39.5 jit_solution(7282324232877635122)
XLA Ops:
  0.6 37.6 %shard_map.95 = (f32[3,16,256]{2,1,0:T(8,128)S(1)}, f32[128,128]{1,0:T(8,128)S(1)}) custom-call(f32[3,16,256]{2,1,0:T(8,128)} %state_h.1, f32[16,256]{1,0:T(8,128)} %temp_h.1, s32[16,256]{1,0:T(8,128)} %land_h.1, bf16[12,64,128]{2,1,0:T(8,128)(2,1)} %bitcast.7, bf16[16,2,3,128,128]{4,3,2,1,0:T(8,128)(2,1)} %w_h.1, s32[3,2,16]{2,1,0:T(2,128)} %bitcast.8, ...), custom_call_target="tpu_custom_call" | custom-call | tf_op jit(solution)/shard_map/pallas_call | solution.py:506
  38.2 0.6 %copy.12 = f32[3,16,256]{2,1,0:T(8,128)} copy(f32[3,16,256]{2,1,0:T(8,128)S(1)} %get-tuple-element.8) | data formatting | bytes 98304
  38.8 0.6 %copy.13 = f32[1,64,2,128]{3,2,1,0:T(2,128)} copy(f32[1,64,2,128]{3,2,1,0:T(2,128)S(1)} %bitcast.6) | data formatting | bytes 131072

commit v6 on v5

--- a/solution.py
+++ b/solution.py
@@ -480,6 +480,8 @@
         extend(own[i], rows_in[0, i], rows_in[1, i], [sides_in[j] for j in range(6)], i, 4) for i in range(4)
     ]
     start_ocean(around, rows, spread, masks, state)
+    all_of(send2, recv2, back_recv).wait()
+    gather_back(listed, recv2, atm_o)
     for copy in fhalo:
         copy.wait_recv()
     push = [
@@ -487,9 +489,7 @@
     ]
     last = subcycles(push, rows, spread, masks, state)
 
-    all_of(send2, recv2, back_recv).wait()
     store_ocean(last, rows, gather, ocean_o)
-    gather_back(listed, recv2, atm_o)
 
     all_of(send1, recv1, tile_send).wait()
     all_of(send2, recv2, back_send).wait()

time: 39.6 us -> 39.5 us (level)
  no operation moved by 1% of the time
where the time goes in v6:
time: 39.5 us; the launch traced here: 39.4 us
  Pallas kernels  37.5 us (95%)
  local copies, waits for them, and re-layouts  1.25 us (3%)
  between operations  0.64 us (2%)
    pallas_call x1, Pallas kernels, shards(): pl.pallas_call(kernel, out_shape=(jax.ShapeDtypeStruct((3, OY, OX), f32),...  37.5 us
    unnamed x2, local copies, waits for them, and re-layouts  1.25 us

profile of v6, /device:TPU:1, one launch (start us, length us, event | category | flops | bytes accessed | tf_op | source)
XLA Modules:
  0.0 39.4 jit_solution(15972207403120961865)
XLA Ops:
  0.6 37.5 %shard_map.95 = (f32[3,16,256]{2,1,0:T(8,128)S(1)}, f32[128,128]{1,0:T(8,128)S(1)}) custom-call(f32[3,16,256]{2,1,0:T(8,128)} %state_h.1, f32[16,256]{1,0:T(8,128)} %temp_h.1, s32[16,256]{1,0:T(8,128)} %land_h.1, bf16[12,64,128]{2,1,0:T(8,128)(2,1)} %bitcast.7, bf16[16,2,3,128,128]{4,3,2,1,0:T(8,128)(2,1)} %w_h.1, s32[3,2,16]{2,1,0:T(2,128)} %bitcast.8, ...), custom_call_target="tpu_custom_call" | custom-call | tf_op jit(solution)/shard_map/pallas_call | solution.py:506
  38.1 0.6 %copy.12 = f32[3,16,256]{2,1,0:T(8,128)} copy(f32[3,16,256]{2,1,0:T(8,128)S(1)} %get-tuple-element.8) | data formatting | bytes 98304
  38.7 0.6 %copy.13 = f32[1,64,2,128]{3,2,1,0:T(2,128)} copy(f32[1,64,2,128]{3,2,1,0:T(2,128)S(1)} %bitcast.6) | data formatting | bytes 131072
